TPU v7x, 32 devices: a whole 2x2x4 slice. The times are simulated.
32 devices in a mesh: tm: 2 (over core), height: 4 (over y, x), chan: 4 (over z).
Axes of the slice: x: 2, y: 2, z: 4, core: 2. Of those that a mesh axis runs over, the one named last changes fastest.
Arguments:
- frames: bfloat16 [4, 16, 256, 128], P('tm', 'height', 'chan'), may hold values from -6 to 6
- grad_out: bfloat16 [4, 16, 256, 128], P('tm', 'height', 'chan'), may hold values from -6 to 6
- weight_one: bfloat16 [256, 3, 3, 3, 256], P('chan'), may hold values from -0.078125 to 0.078125
- weight_two: bfloat16 [256, 3, 3, 3, 256], P('chan'), may hold values from -0.078125 to 0.078125
Outputs:
- grad_frames: bfloat16 [4, 16, 256, 128], P('tm', 'height', 'chan')
- grad_one: float32 [256, 3, 3, 3, 256], P('chan')
- grad_two: float32 [256, 3, 3, 3, 256], P('chan')
All inputs are finite; a program needn't handle non-finite values.
Results may differ from a plain program's by a relative error of at most 0.015.
Values may be sent and summed in bfloat16 or wider, within the bound.
A program may use at most 128 MiB of HBM per device.

v0:
```python
import jax
import jax.numpy as jnp
from jax import lax
from jax.sharding import PartitionSpec as P


def passed_along(block, axis, distance):
    devices = range(lax.axis_size(axis))
    route = [(i - distance, i) for i in devices if i - distance in devices]
    return lax.ppermute(block, axis, route)


def extended(cells, sides, width):
    for axis, dim in sides:
        count = lax.axis_size(axis)
        ends = count - 1
        head = lax.slice_in_dim(cells, 0, width, axis=dim)
        tail = lax.slice_in_dim(cells, cells.shape[dim] - width, cells.shape[dim], axis=dim)
        cells = jnp.concatenate(
            [
                lax.ppermute(tail, axis, [(i, (i + 1) % count) for i in range(ends)]),
                cells,
                lax.ppermute(head, axis, [((i + 1) % count, i) for i in range(ends)]),
            ],
            axis=dim,
        )
    return cells


def product(form, left, right):
    return jnp.einsum(form, left, right, preferred_element_type=jnp.float32)


def shift_cols(block, offset):
    if offset == 0:
        return block
    edge = jnp.zeros(block.shape[:3] + (1,), block.dtype)
    if offset > 0:
        return jnp.concatenate([block[..., 1:], edge], 3)
    return jnp.concatenate([edge, block[..., :-1]], 3)


def forward_taps(padded, weight):
    frame_count = padded.shape[0] - 2
    row_count = padded.shape[1] - 2
    col_count = padded.shape[3]
    summed = jnp.zeros((frame_count, row_count, weight.shape[0], col_count), jnp.float32)
    for col_tap in range(3):
        partial_sum = jnp.zeros((frame_count, row_count, weight.shape[0], col_count), jnp.float32)
        for time_tap in range(3):
            for row_tap in range(3):
                window = padded[time_tap : time_tap + frame_count, row_tap : row_tap + row_count]
                partial_sum = partial_sum + product(
                    "frcw,oc->frow", window, weight[:, time_tap, row_tap, col_tap, :]
                )
        summed = summed + shift_cols(partial_sum, col_tap - 1)
    return summed


def backward_taps(padded, weight):
    frame_count = padded.shape[0] - 2
    row_count = padded.shape[1] - 2
    col_count = padded.shape[3]
    summed = jnp.zeros((frame_count, row_count, weight.shape[4], col_count), jnp.float32)
    for col_tap in range(3):
        partial_sum = jnp.zeros((frame_count, row_count, weight.shape[4], col_count), jnp.float32)
        for time_tap in range(3):
            for row_tap in range(3):
                window = padded[
                    2 - time_tap : 2 - time_tap + frame_count, 2 - row_tap : 2 - row_tap + row_count
                ]
                partial_sum = partial_sum + product(
                    "frow,oc->frcw", window, weight[:, time_tap, row_tap, col_tap, :]
                )
        summed = summed + shift_cols(partial_sum, 1 - col_tap)
    return summed


def forward_filter(padded, gradient):
    frame_count, row_count, out_width, col_count = gradient.shape
    moved = [shift_cols(gradient, 1 - col_tap) for col_tap in range(3)]
    pieces = []
    for time_tap in range(3):
        for row_tap in range(3):
            window = padded[time_tap : time_tap + frame_count, row_tap : row_tap + row_count]
            for col_tap in range(3):
                pieces.append(product("frcw,frow->oc", window, moved[col_tap]))
    return jnp.stack(pieces, 1).reshape(out_width, 3, 3, 3, padded.shape[2])


def backward_filter(source, padded):
    frame_count, row_count, in_width, col_count = source.shape
    moved = [shift_cols(padded, 1 - col_tap) for col_tap in range(3)]
    pieces = []
    for time_tap in range(3):
        for row_tap in range(3):
            for col_tap in range(3):
                window = moved[col_tap][
                    2 - time_tap : 2 - time_tap + frame_count, 2 - row_tap : 2 - row_tap + row_count
                ]
                pieces.append(product("frcw,frow->oc", source, window))
    return jnp.stack(pieces, 1).reshape(padded.shape[2], 3, 3, 3, in_width)


def on_device(frames, grad_out, weight_one, weight_two):
    earlier = passed_along(frames, "tm", 1)
    frames_time = jnp.concatenate([earlier, frames], 0)
    frames_rows = extended(frames_time, (("height", 1),), 1)
    frames_panel = lax.all_gather(frames_rows, "chan", axis=2, tiled=True)
    pre = forward_taps(frames_panel, weight_one)
    act = jax.nn.silu(pre).astype(jnp.bfloat16)
    later = passed_along(grad_out, "tm", -1)
    grads_time = jnp.concatenate([grad_out, later], 0)
    grads_padded = extended(grads_time, (("height", 1),), 1)
    act_full = lax.all_gather(act, "chan", axis=2, tiled=True)
    part_two = backward_filter(act_full, grads_padded)
    sigmoid_pre = jax.nn.sigmoid(pre)
    grad_act = lax.psum_scatter(
        backward_taps(grads_padded, weight_two), "chan", scatter_dimension=2, tiled=True
    )
    grad_pre = (grad_act * sigmoid_pre * (1.0 + pre * (1.0 - sigmoid_pre))).astype(jnp.bfloat16)
    pre_later = passed_along(grad_pre, "tm", -1)
    pre_time = jnp.concatenate([grad_pre, pre_later], 0)
    pre_padded = extended(pre_time, (("height", 1),), 1)
    grad_frames = lax.psum_scatter(
        backward_taps(pre_padded, weight_one).astype(jnp.bfloat16),
        "chan",
        scatter_dimension=2,
        tiled=True,
    )
    part_one = forward_filter(frames_panel, grad_pre)
    grad_one, grad_two = lax.psum((part_one, part_two), ("tm", "height"))
    return (grad_frames, grad_one, grad_two)


def solution(mesh):
    in_specs = (
        P("tm", "height", "chan", None),
        P("tm", "height", "chan", None),
        P("chan", None, None, None, None),
        P("chan", None, None, None, None),
    )
    out_specs = (
        P("tm", "height", "chan", None),
        P("chan", None, None, None, None),
        P("chan", None, None, None, None),
    )
    return jax.shard_map(
        on_device, mesh=mesh, in_specs=in_specs, out_specs=out_specs, check_vma=False
    )
```

profile of v0, /device:TPU:0, one launch (start us, length us, event | category | flops | bytes accessed | tf_op | source)
XLA Modules:
  0.0 316.6 jit_solution(16765228953827332015)
XLA Ops:
  7.2 1.4 collective-permute-start
  8.7 1.3 convolution_bitcast_fusion.21
  12.7 4.8 %collective-permute-start.2 = (bf16[4,1,64,128]{3,2,1,0:T(8,128)(2,1)S(1)}, bf16[4,1,64,128]{3,2,1,0:T(8,128)(2,1)S(1)}, u32[]{:S(2)}, u32[]{:S(2)}) collective-permute-start(bf16[4,1,64,128]{3,2,1,0:T(8,128)(2,1)S(1)} %get-tuple-element.20), channel_id=1, source_target_pairs={{0,4},{4,8},{8,12},{1,5},{5,9},{9,13},{2,6},{6,10},{10,14},{3,7},{... | collective-permute-start | bytes 196616 | tf_op jit(solution)/shard_map/ppermute | solution.py:21
  17.5 1.3 collective-permute-start.1
  21.2 3.0 collective-permute-done.1
  35.1 1.6 fusion.36
  36.7 1.3 copy.128
  38.1 1.9 collective-permute-start.3
  41.0 4.3 %collective-permute-start.4 = (bf16[4,1,64,128]{3,2,1,0:T(8,128)(2,1)S(1)}, bf16[4,1,64,128]{3,2,1,0:T(8,128)(2,1)S(1)}, u32[]{:S(2)}, u32[]{:S(2)}) collective-permute-start(bf16[4,1,64,128]{3,2,1,0:T(8,128)(2,1)S(1)} %get-tuple-element.17), channel_id=1, source_target_pairs={{0,4},{4,8},{8,12},{1,5},{5,9},{9,13},{2,6},{6,10},{10,14},{3,7},{... | collective-permute-start | bytes 196616 | tf_op jit(solution)/shard_map/ppermute | solution.py:21
  45.3 1.3 collective-permute-start.5
  47.2 4.3 %collective-permute-done.5 = bf16[4,1,64,128]{3,2,1,0:T(8,128)(2,1)S(1)} collective-permute-done((bf16[4,1,64,128]{3,2,1,0:T(8,128)(2,1)S(1)}, bf16[4,1,64,128]{3,2,1,0:T(8,128)(2,1)S(1)}, u32[]{:S(2)}, u32[]{:S(2)}) %collective-permute-start.5) | collective-permute-done | bytes 65568 | tf_op jit(solution)/shard_map/ppermute | solution.py:23
  54.0 37.2 %all-reduce.17.cloned.1.call-done = f32[2,4,256,128]{3,1,0,2:T(4,128)} async-done(((f32[2,4,256,128]{3,1,0,2:T(4,128)}), f32[2,4,256,128]{3,1,0,2:T(4,128)}) %all-reduce.17.cloned.1.call-update) | async-done | bytes 1048592
  91.2 1.7 constant_dynamic-slice_fusion.1
  92.9 37.1 %all-gather.2.cloned.1.call-done = bf16[4,6,256,128]{3,2,1,0:T(8,128)(2,1)} async-done(((bf16[4,6,64,128]{3,2,1,0:T(8,128)(2,1)}), bf16[4,6,256,128]{3,2,1,0:T(8,128)(2,1)}) %all-gather.2.cloned.1.call-update) | async-done | bytes 1572880 | tf_op jit(solution)/shard_map/all_gather | solution.py:109
  129.9 1.4 fusion.148
  131.3 1.3 convolution_add_fusion.13
  140.3 1.3 collective-permute-start.6
  142.7 16.1 %all_gather.7 = bf16[2,4,256,128]{3,1,0,2:T(4,128)(2,1)S(1)} all-gather(bf16[2,4,64,128]{3,1,0,2:T(4,128)(2,1)S(1)} %copy.131), channel_id=1, replica_groups=mesh['tm'=2,'height'=4,'chan'=4] {'chan'}, dimensions={2}, use_global_device_ids=true | all-gather | bytes 655360 | tf_op jit(solution)/shard_map/all_gather | solution.py:115
  173.4 3.4 %collective-permute-start.8 = (bf16[4,1,64,128]{3,2,1,0:T(8,128)(2,1)S(1)}, bf16[4,1,64,128]{3,2,1,0:T(8,128)(2,1)S(1)}, u32[]{:S(2)}, u32[]{:S(2)}) collective-permute-start(bf16[4,1,64,128]{3,2,1,0:T(8,128)(2,1)S(1)} %get-tuple-element.15), channel_id=1, source_target_pairs={{0,4},{4,8},{8,12},{1,5},{5,9},{9,13},{2,6},{6,10},{10,14},{3,7},{... | collective-permute-start | bytes 196616 | tf_op jit(solution)/shard_map/ppermute | solution.py:21
  176.8 1.5 collective-permute-start.7
  181.0 2.0 collective-permute-done.7
  193.1 34.6 %all-reduce.19.cloned.1.call-done = bf16[2,4,256,128]{3,1,0,2:T(4,128)(2,1)} async-done(((bf16[2,4,256,128]{3,1,0,2:T(4,128)(2,1)}), bf16[2,4,256,128]{3,1,0,2:T(4,128)(2,1)}) %all-reduce.19.cloned.1.call-update) | async-done | bytes 524304
  229.3 76.5 %all-reduce.21.cloned.1.call-done = (f32[64,3,3,3,256]{4,0,3,2,1:T(8,128)}, f32[64,3,3,3,256]{4,0,3,2,1:T(8,128)}) async-done(((f32[64,3,3,3,256]{4,0,3,2,1:T(8,128)}, f32[64,3,3,3,256]{4,0,3,2,1:T(8,128)}), (f32[64,3,3,3,256]{4,0,3,2,1:T(8,128)}, f32[64,3,3,3,256]{4,0,3,2,1:T(8,128)})) %all-reduce.21.cloned.1.call-update) | async-done | bytes 3538960 | tf_op jit(solution)/shard_map/psum | solution.py:132
  305.9 3.0 copy.391
  (185 shorter events, 57.9 us)
Async XLA Ops:
  7.2 4.1 %copy-start.2 = (bf16[2,4,64,128]{3,2,1,0:T(8,128)(2,1)S(1)}, bf16[2,4,64,128]{3,2,1,0:T(8,128)(2,1)}, u32[]{:S(2)}) copy-start(bf16[2,4,64,128]{3,2,1,0:T(8,128)(2,1)} %param.5) | copy-start | bytes 393220
  7.2 4.1 %copy-start.6 = (bf16[64,3,3,3,256]{4,0,3,2,1:T(8,128)(2,1)S(1)}, bf16[64,3,3,3,256]{4,0,3,2,1:T(8,128)(2,1)}, u32[]{:S(2)}) copy-start(bf16[64,3,3,3,256]{4,0,3,2,1:T(8,128)(2,1)} %param.7) | copy-start | bytes 2654212
  7.2 84.0 %all-reduce.17.cloned.1.call-start = ((), (), s32[]{:S(2)}) async-start(), calls=%async_computation.1 | async-start | bytes 2097152
  7.2 4.4 %collective-permute-start = (bf16[2,4,64,128]{3,2,1,0:T(8,128)(2,1)}, bf16[2,4,64,128]{3,2,1,0:T(8,128)(2,1)S(1)}, u32[]{:S(2)}, u32[]{:S(2)}) collective-permute-start(bf16[2,4,64,128]{3,2,1,0:T(8,128)(2,1)} %param.5), channel_id=1, source_target_pairs={{16,0},{17,1},{18,2},{19,3},{20,4},{21,5},{22,6},{23,7},{24,8},{25... | collective-permute-start | bytes 393224 | tf_op jit(solution)/shard_map/ppermute | solution.py:10
  12.7 7.2 %collective-permute-start.2 = (bf16[4,1,64,128]{3,2,1,0:T(8,128)(2,1)S(1)}, bf16[4,1,64,128]{3,2,1,0:T(8,128)(2,1)S(1)}, u32[]{:S(2)}, u32[]{:S(2)}) collective-permute-start(bf16[4,1,64,128]{3,2,1,0:T(8,128)(2,1)S(1)} %get-tuple-element.20), channel_id=1, source_target_pairs={{0,4},{4,8},{8,12},{1,5},{5,9},{9,13},{2,6},{6,10},{10,14},{3,7},{... | collective-permute-start | bytes 196616 | tf_op jit(solution)/shard_map/ppermute | solution.py:21
  17.5 6.7 %collective-permute-start.1 = (bf16[4,1,64,128]{3,2,1,0:T(8,128)(2,1)S(1)}, bf16[4,1,64,128]{3,2,1,0:T(8,128)(2,1)S(1)}, u32[]{:S(2)}, u32[]{:S(2)}) collective-permute-start(bf16[4,1,64,128]{3,2,1,0:T(8,128)(2,1)S(1)} %get-tuple-element.19), channel_id=1, source_target_pairs={{4,0},{8,4},{12,8},{5,1},{9,5},{13,9},{6,2},{10,6},{14,10},{7,3},{... | collective-permute-start | bytes 196616 | tf_op jit(solution)/shard_map/ppermute | solution.py:23
  36.7 1.4 copy-start.8
  38.0 14.5 %copy-start.9 = (u32[32]{0:T(128)S(1)}, u32[32]{0:T(128)}, u32[]{:S(2)}) copy-start(u32[32]{0:T(128)} %constant.32) | copy-start | bytes 388
  38.0 91.9 %all-gather.2.cloned.1.call-start = ((), (), s32[]{:S(2)}) async-start(), calls=%async_computation | async-start | bytes 1966080 | tf_op jit(solution)/shard_map/all_gather | solution.py:109
  38.1 2.8 collective-permute-start.3
  41.0 6.2 %collective-permute-start.4 = (bf16[4,1,64,128]{3,2,1,0:T(8,128)(2,1)S(1)}, bf16[4,1,64,128]{3,2,1,0:T(8,128)(2,1)S(1)}, u32[]{:S(2)}, u32[]{:S(2)}) collective-permute-start(bf16[4,1,64,128]{3,2,1,0:T(8,128)(2,1)S(1)} %get-tuple-element.17), channel_id=1, source_target_pairs={{0,4},{4,8},{8,12},{1,5},{5,9},{9,13},{2,6},{6,10},{10,14},{3,7},{... | collective-permute-start | bytes 196616 | tf_op jit(solution)/shard_map/ppermute | solution.py:21
  45.3 6.2 %collective-permute-start.5 = (bf16[4,1,64,128]{3,2,1,0:T(8,128)(2,1)S(1)}, bf16[4,1,64,128]{3,2,1,0:T(8,128)(2,1)S(1)}, u32[]{:S(2)}, u32[]{:S(2)}) collective-permute-start(bf16[4,1,64,128]{3,2,1,0:T(8,128)(2,1)S(1)} %get-tuple-element.18), channel_id=1, source_target_pairs={{4,0},{8,4},{12,8},{5,1},{9,5},{13,9},{6,2},{10,6},{14,10},{7,3},{... | collective-permute-start | bytes 196616 | tf_op jit(solution)/shard_map/ppermute | solution.py:23
  52.3 175.4 %all-reduce.19.cloned.1.call-start = ((), (), s32[]{:S(2)}) async-start(), calls=%async_computation.2 | async-start | bytes 1048576
  129.9 2.8 copy-start
  131.3 3.3 %copy-start.1 = (bf16[64,3,3,3,256]{4,0,3,2,1:T(8,128)(2,1)S(1)}, bf16[64,3,3,3,256]{4,0,3,2,1:T(8,128)(2,1)}, u32[]{:S(2)}) copy-start(bf16[64,3,3,3,256]{4,0,3,2,1:T(8,128)(2,1)} %param.6) | copy-start | bytes 2654212
  138.9 1.0 copy-start.7
  140.3 33.1 %collective-permute-start.6 = (bf16[2,4,64,128]{3,2,1,0:T(8,128)(2,1)S(1)}, bf16[2,4,64,128]{3,2,1,0:T(8,128)(2,1)S(1)}, u32[]{:S(2)}, u32[]{:S(2)}) collective-permute-start(bf16[2,4,64,128]{3,2,1,0:T(8,128)(2,1)S(1)} %get-tuple-element.14), channel_id=1, source_target_pairs={{16,0},{17,1},{18,2},{19,3},{20,4},{21,5},{22,6},{23,7},{24,8},{25... | collective-permute-start | bytes 393224 | tf_op jit(solution)/shard_map/ppermute | solution.py:10
  166.5 1.4 copy-start.3
  173.4 5.9 %copy-start.5 = (f32[64,27,256]{2,0,1:T(8,128)}, f32[64,27,256]{2,0,1:T(8,128)S(1)}, u32[]{:S(2)}) copy-start(f32[64,27,256]{2,0,1:T(8,128)S(1)} %fusion.73) | copy-start | bytes 5308420
  173.4 6.9 %collective-permute-start.8 = (bf16[4,1,64,128]{3,2,1,0:T(8,128)(2,1)S(1)}, bf16[4,1,64,128]{3,2,1,0:T(8,128)(2,1)S(1)}, u32[]{:S(2)}, u32[]{:S(2)}) collective-permute-start(bf16[4,1,64,128]{3,2,1,0:T(8,128)(2,1)S(1)} %get-tuple-element.15), channel_id=1, source_target_pairs={{0,4},{4,8},{8,12},{1,5},{5,9},{9,13},{2,6},{6,10},{10,14},{3,7},{... | collective-permute-start | bytes 196616 | tf_op jit(solution)/shard_map/ppermute | solution.py:21
  176.8 6.2 %collective-permute-start.7 = (bf16[4,1,64,128]{3,2,1,0:T(8,128)(2,1)S(1)}, bf16[4,1,64,128]{3,2,1,0:T(8,128)(2,1)S(1)}, u32[]{:S(2)}, u32[]{:S(2)}) collective-permute-start(bf16[4,1,64,128]{3,2,1,0:T(8,128)(2,1)S(1)} %get-tuple-element.16), channel_id=1, source_target_pairs={{4,0},{8,4},{12,8},{5,1},{9,5},{13,9},{6,2},{10,6},{14,10},{7,3},{... | collective-permute-start | bytes 196616 | tf_op jit(solution)/shard_map/ppermute | solution.py:23
  190.3 115.6 %all-reduce.21.cloned.1.call-start = ((), (), s32[]{:S(2)}) async-start(), calls=%async_computation.3 | async-start | bytes 7077888 | tf_op jit(solution)/shard_map/psum | solution.py:132
  305.9 3.0 copy-start.4
Sparse Core Ops, SparseCore 0:
  38.1 53.0 all-reduce.16
  93.4 36.4 all-gather.1
  190.4 37.2 all-reduce.18
  231.9 73.9 all-reduce.20
where the time goes:
time: 318 us; the launch traced here: 317 us
  waiting for transfers between devices  196 us (62%)
  matrix products  53.9 us (17%)
  starting transfers between devices  21.6 us (7%)
  blocking collectives  16.1 us (5%)
  between operations  15.3 us (5%)
  local copies, waits for them, and re-layouts  11.5 us (4%)
    psum x1, waiting for transfers between devices, on_device(): grad_one, grad_two = lax.psum((part_one, part_two), ('tm', 'height'))  76.5 us
    unnamed x6, waiting for transfers between devices  71.8 us
    dot_general x135, matrix products, product(): return jnp.einsum(form, left, right, preferred_element_type=jnp.float32)  53.9 us
    all_gather x1, waiting for transfers between devices, on_device(): frames_panel = lax.all_gather(frames_rows, 'chan', axis=2, tiled=True)  37.1 us
    all_gather x1, blocking collectives, on_device(): act_full = lax.all_gather(act, 'chan', axis=2, tiled=True)  16.1 us
    ppermute x3, starting transfers between devices, extended(): lax.ppermute(tail, axis, [(i, (i + 1) % count) for i in range(ends)])  12.5 us
    ppermute x3, waiting for transfers between devices, extended(): lax.ppermute(head, axis, [((i + 1) % count, i) for i in range(ends)])  9.27 us
    unnamed x28, local copies, waits for them, and re-layouts  8.45 us
  transfers between devices with their start and end apart: 13, of which 9 were waited for; matrix products, arithmetic and copies ran while one was open for 10% of the time, Pallas kernels for 0%

commit v1 on v0

v1 whole, which is shorter than its diff:
```python
import functools

import jax
import jax.numpy as jnp
from jax import lax
from jax.experimental import pallas as pl
from jax.experimental.pallas import tpu as pltpu
from jax.sharding import PartitionSpec as P

BF16 = jnp.bfloat16
F32 = jnp.float32
MESH = pl.DeviceIdType.MESH
HALO = 5


def moved_cols(block, offset):
    lane = lax.broadcasted_iota(jnp.int32, block.shape, 1)
    cols = block.shape[1]
    if offset > 0:
        return jnp.where(lane == cols - 1, 0.0, pltpu.roll(block, cols - 1, 1))
    return jnp.where(lane == 0, 0.0, pltpu.roll(block, 1, 1))


def kernel(
    sizes,
    frames, gout, w1, w2,
    gf_out, g1_out, g2_out,
    x, g, gsh, gp, gpsh, w1t, w2t, pre, ga, gain, act, gf, gfin,
    town, tsend, trecv, hown, hsend, hrecv, fin,
    z_send, z_recv, xh_send, xh_recv, gh_send, gh_recv,
    t_send, t_recv, h_send, h_recv, a_send, a_recv, p_send, p_recv,
):
    T, H, Z = sizes
    F, R, C, J = frames.shape
    CC = C * Z
    O = C
    slabs = F * R
    part = 3 * O // H
    tm, h, z = lax.axis_index("tm"), lax.axis_index("height"), lax.axis_index("chan")
    pair = tm + 1 - 2 * lax.rem(tm, 2)
    parity = lax.rem(tm, 2)

    up, down = h > 0, h < H - 1
    has_prev, has_next = tm > 0, tm < T - 1

    def zpeer(d):
        return {"chan": lax.rem(z + d, Z)}

    def hpeer(d):
        return {"height": lax.rem(h + d, H)}

    barrier = pltpu.get_barrier_semaphore()
    for d in range(1, Z):
        pl.semaphore_signal(barrier, inc=1, device_id=zpeer(d), device_id_type=MESH)
    for d in range(1, H):
        pl.semaphore_signal(barrier, inc=1, device_id=hpeer(d), device_id_type=MESH)
    for cond_t, dt in ((has_prev, -1), (has_next, 1)):
        @pl.when(cond_t)
        def _(dt=dt):
            pl.semaphore_signal(barrier, inc=1, device_id={"tm": tm + dt}, device_id_type=MESH)
        for cond_h, dh in ((up, -1), (down, 1)):
            @pl.when(jnp.logical_and(cond_t, cond_h))
            def _(dt=dt, dh=dh):
                pl.semaphore_signal(
                    barrier, inc=1, device_id={"tm": tm + dt, "height": h + dh}, device_id_type=MESH
                )
    n_t = jnp.where(has_prev, 1, 0) + jnp.where(has_next, 1, 0)
    n_h = jnp.where(up, 1, 0) + jnp.where(down, 1, 0)
    pl.semaphore_wait(barrier, (Z - 1) + (H - 1) + n_t + n_t * n_h)

    pending = []

    def remote(src, dst, ssem, rsem, dev):
        return pltpu.make_async_remote_copy(
            src_ref=src, dst_ref=dst, send_sem=ssem, recv_sem=rsem, device_id=dev, device_id_type=MESH
        )

    def send(copy):
        copy.start()
        pending.append((None, copy))
        return copy

    def halo(ext, dt, chan_slice, ssems, rsems):
        o0, f0 = (F, 0) if dt > 0 else (0, F)
        to_t = has_next if dt > 0 else has_prev
        from_t = has_prev if dt > 0 else has_next

        def at(frame, row, rows):
            return ext.at[pl.ds(frame, F), pl.ds(row, rows), chan_slice, :]

        plan = [
            (to_t, from_t, at(o0, 1, R), at(f0, 1, R), {"tm": tm + dt}),
            (down, up, at(o0, R, 1), at(o0, 0, 1), {"height": h + 1}),
            (up, down, at(o0, 1, 1), at(o0, R + 1, 1), {"height": h - 1}),
            (
                jnp.logical_and(to_t, down), jnp.logical_and(from_t, up),
                at(o0, R, 1), at(f0, 0, 1), {"tm": tm + dt, "height": h + 1},
            ),
            (
                jnp.logical_and(to_t, up), jnp.logical_and(from_t, down),
                at(o0, 1, 1), at(f0, R + 1, 1), {"tm": tm + dt, "height": h - 1},
            ),
        ]
        waits = []
        for k, (go, come, src, dst, dev) in enumerate(plan):
            copy = remote(src, dst, ssems[k], rsems[k], dev)
            pl.when(go)(copy.start)
            pending.append((go, copy))
            waits.append((come, copy))
        return waits

    def arrive(waits):
        for come, copy in waits:
            pl.when(come)(copy.wait_recv)

    def zero_edges(ext, dt):
        f0 = 0 if dt > 0 else F
        blank = jnp.logical_not(has_prev if dt > 0 else has_next)

        @pl.when(blank)
        def _():
            ext[f0 : f0 + F] = jnp.zeros((F,) + ext.shape[1:], ext.dtype)

        @pl.when(jnp.logical_not(up))
        def _():
            ext[:, 0] = jnp.zeros((2 * F,) + ext.shape[2:], ext.dtype)

        @pl.when(jnp.logical_not(down))
        def _():
            ext[:, R + 1] = jnp.zeros((2 * F,) + ext.shape[2:], ext.dtype)

    def chunk(index):
        return pl.ds(pl.multiple_of(index * C, C), C)

    mine = chunk(z)

    z_frames = [
        send(remote(
            frames, x.at[pl.ds(F, F), pl.ds(1, R), mine, :],
            z_send.at[0, d - 1], z_recv.at[0, d - 1], zpeer(d),
        ))
        for d in range(1, Z)
    ]
    g[0:F, 1 : R + 1] = gout[...]
    g_waits = halo(
        g, -1, pl.ds(0, C), [gh_send.at[0, k] for k in range(HALO)], [gh_recv.at[0, k] for k in range(HALO)]
    )
    x[F : 2 * F, 1 : R + 1, mine, :] = frames[...]
    x_waits = [halo(
        x, 1, mine, [xh_send.at[0, k] for k in range(HALO)], [xh_recv.at[0, k] for k in range(HALO)]
    )]
    zero_edges(g, -1)
    zero_edges(gp, -1)
    zero_edges(x, 1)

    @pl.loop(0, 9)
    def _(ab):
        w2t[ab] = w2[ab].T
        w1t[ab] = w1[ab].T

    def spread(src, dst, t, i):
        wide = src[t, i].astype(F32)
        dst[t, i, 0:O] = moved_cols(wide, 1).astype(BF16)
        dst[t, i, O : 2 * O] = src[t, i]
        dst[t, i, 2 * O : 3 * O] = moved_cols(wide, -1).astype(BF16)

    def back(source, weight, out):
        @pl.loop(0, slabs // 2)
        def _(s):
            t, i = s // (R // 2), 2 * lax.rem(s, R // 2)
            total = jnp.zeros((CC, 2 * J), F32)
            for a in range(3):
                for b in range(3):
                    window = jnp.concatenate(
                        [source[t + 2 - a, i + 2 - b], source[t + 2 - a, i + 3 - b]], 1
                    )
                    total += jnp.dot(weight[a * 3 + b], window, preferred_element_type=F32)
            out[2 * s] = total[:, :J].astype(BF16)
            out[2 * s + 1] = total[:, J:].astype(BF16)

    def scatter(phase, src, dst):
        return [
            send(remote(
                src.at[:, chunk(lax.rem(z + d, Z)), :], dst.at[d - 1],
                z_send.at[phase, d - 1], z_recv.at[phase, d - 1], zpeer(d),
            ))
            for d in range(1, Z)
        ]

    arrive(g_waits)

    @pl.loop(0, 2 * F * (R + 2))
    def _(s):
        spread(g, gsh, s // (R + 2), lax.rem(s, R + 2))

    back(gsh, w2t, ga)
    z_ga = scatter(1, ga, gain)

    for d in range(1, Z):
        z_frames[d - 1].wait_recv()
        x_waits.append(halo(
            x, 1, chunk(lax.rem(z - d + Z, Z)),
            [xh_send.at[d, k] for k in range(HALO)], [xh_recv.at[d, k] for k in range(HALO)],
        ))
    for waits in x_waits:
        arrive(waits)

    @pl.loop(0, slabs // 2)
    def _(s):
        t, i = s // (R // 2), 2 * lax.rem(s, R // 2)
        total = jnp.zeros((3 * O, 2 * J), F32)
        for a in range(3):
            for b in range(3):
                window = jnp.concatenate([x[t + a, i + b], x[t + a, i + b + 1]], 1)
                total += jnp.dot(w1[a * 3 + b], window, preferred_element_type=F32)
        for half in range(2):
            cols = total[:, half * J : (half + 1) * J]
            value = moved_cols(cols[0:O], -1) + cols[O : 2 * O] + moved_cols(cols[2 * O :], 1)
            pre[2 * s + half] = value
            act[2 * s + half, mine, :] = (value * jax.nn.sigmoid(value)).astype(BF16)

    z_act = [
        send(remote(
            act.at[:, mine, :], act.at[:, mine, :],
            z_send.at[2, d - 1], z_recv.at[2, d - 1], zpeer(d),
        ))
        for d in range(1, Z)
    ]

    for copy in z_ga:
        copy.wait_recv()

    @pl.loop(0, slabs)
    def _(s):
        t, i = s // R, lax.rem(s, R)
        total = ga[s, mine, :].astype(F32)
        for d in range(1, Z):
            total += gain[d - 1, s].astype(F32)
        value = pre[s]
        sig = jax.nn.sigmoid(value)
        gp[t, i + 1] = (total * sig * (1.0 + value * (1.0 - sig))).astype(BF16)

    gp_waits = halo(
        gp, -1, pl.ds(0, C), [gh_send.at[1, k] for k in range(HALO)], [gh_recv.at[1, k] for k in range(HALO)]
    )

    @pl.loop(0, slabs)
    def _(s):
        spread(gp, gpsh, s // R, lax.rem(s, R) + 1)

    def keep(f, ab, value):
        left, right = value[:, :J], value[:, J:]
        town[f, ab] = jnp.where(parity == 0, left, right)
        tsend[f, ab] = jnp.where(parity == 0, right, left).astype(BF16)

    def to_pair(f):
        return send(remote(tsend.at[f], trecv.at[f], t_send.at[f], t_recv.at[f], {"tm": pair}))

    nt = (((1,), (1,)), ((), ()))

    def row_of(source, t0, i0):
        return jnp.concatenate([source[t0 + s // R, i0 + s % R] for s in range(slabs)], 1)

    @pl.loop(0, 9)
    def _(ab):
        left = row_of(gpsh, 0, 1)
        right = row_of(x, ab // 3, lax.rem(ab, 3))
        keep(0, ab, lax.dot_general(left, right, nt, preferred_element_type=F32))

    t_copies = [to_pair(0)]

    arrive(gp_waits)

    @pl.loop(0, F * (R + 2))
    def _(s):
        spread(gp, gpsh, F + s // (R + 2), lax.rem(s, R + 2))

    for t in range(F):
        for i in (0, R + 1):
            spread(gp, gpsh, t, i)
    back(gpsh, w1t, gf)
    z_gf = scatter(3, gf, gfin)

    def from_pair(f):
        t_copies[f].wait_recv()

        @pl.loop(0, 9)
        def _(ab):
            total = town[f, ab] + trecv[f, ab].astype(F32)
            hown[f, ab] = total
            hsend[f, ab] = total.astype(BF16)

        return [
            send(remote(
                hsend.at[f, :, pl.ds(pl.multiple_of(lax.rem(h + d, H) * part, part), part), :],
                hrecv.at[f, d - 1],
                h_send.at[f, d - 1], h_recv.at[f, d - 1], hpeer(d),
            ))
            for d in range(1, H)
        ]

    def from_rows(f, copies):
        for copy in copies:
            copy.wait_recv()
        rows = pl.ds(pl.multiple_of(h * part, part), part)

        @pl.loop(0, 9)
        def _(ab):
            total = hown[f, ab, rows, :]
            for d in range(1, H):
                total += hrecv[f, d - 1, ab].astype(F32)
            fin[f, parity, ab, rows, :] = total.astype(BF16)

        block = fin.at[f, parity, :, rows, :]
        return [
            send(remote(block, block, a_send.at[f, d - 1], a_recv.at[f, d - 1], hpeer(d)))
            for d in range(1, H)
        ]

    def to_other(f, copies):
        for copy in copies:
            copy.wait_recv()
        half = fin.at[f, parity]
        return send(remote(half, half, p_send.at[f], p_recv.at[f], {"tm": pair}))

    h_one = from_pair(0)

    for copy in z_act:
        copy.wait_recv()

    @pl.loop(0, 9)
    def _(ab):
        left = row_of(gsh, 2 - ab // 3, 2 - lax.rem(ab, 3))
        right = jnp.concatenate([act[s] for s in range(slabs)], 1)
        keep(1, ab, lax.dot_general(left, right, nt, preferred_element_type=F32))

    t_copies.append(to_pair(1))
    a_one = from_rows(0, h_one)
    h_two = from_pair(1)
    p_one = to_other(0, a_one)
    a_two = from_rows(1, h_two)

    for copy in z_gf:
        copy.wait_recv()

    @pl.loop(0, slabs)
    def _(s):
        total = gf[s, mine, :].astype(F32)
        for d in range(1, Z):
            total += gfin[d - 1, s].astype(F32)
        gf_out[s // R, lax.rem(s, R)] = total.astype(BF16)

    p_two = to_other(1, a_two)
    p_one.wait_recv()
    g1_out[...] = fin[0]
    p_two.wait_recv()
    g2_out[...] = fin[1]

    for go, copy in pending:
        if go is None:
            copy.wait_send()
        else:
            pl.when(go)(copy.wait_send)


def on_device(sizes, frames, grad_out, weight_one, weight_two):
    T, H, Z = sizes
    F, R, C, J = frames.shape
    CC, slabs, part = C * Z, F * R, 3 * C // H

    def taps_first(weight):
        return weight.transpose(1, 2, 3, 0, 4).reshape(9, 3 * C, CC)

    dma = pltpu.SemaphoreType.DMA
    ext = (2 * F, R + 2)
    scratch = [
        pltpu.VMEM(ext + (CC, J), BF16),
        pltpu.VMEM(ext + (C, J), BF16),
        pltpu.VMEM(ext + (3 * C, J), BF16),
        pltpu.VMEM(ext + (C, J), BF16),
        pltpu.VMEM(ext + (3 * C, J), BF16),
        pltpu.VMEM((9, CC, 3 * C), BF16),
        pltpu.VMEM((9, CC, 3 * C), BF16),
        pltpu.VMEM((slabs, C, J), F32),
        pltpu.VMEM((slabs, CC, J), BF16),
        pltpu.VMEM((Z - 1, slabs, C, J), BF16),
        pltpu.VMEM((slabs, CC, J), BF16),
        pltpu.VMEM((slabs, CC, J), BF16),
        pltpu.VMEM((Z - 1, slabs, C, J), BF16),
        pltpu.VMEM((2, 9, 3 * C, CC // 2), F32),
        pltpu.VMEM((2, 9, 3 * C, CC // 2), BF16),
        pltpu.VMEM((2, 9, 3 * C, CC // 2), BF16),
        pltpu.VMEM((2, 9, 3 * C, CC // 2), F32),
        pltpu.VMEM((2, 9, 3 * C, CC // 2), BF16),
        pltpu.VMEM((2, H - 1, 9, part, CC // 2), BF16),
        pltpu.VMEM((2, 2, 9, 3 * C, CC // 2), BF16),
        dma((4, Z - 1)), dma((4, Z - 1)),
        dma((Z, HALO)), dma((Z, HALO)),
        dma((2, HALO)), dma((2, HALO)),
        dma((2,)), dma((2,)),
        dma((2, H - 1)), dma((2, H - 1)),
        dma((2, H - 1)), dma((2, H - 1)),
        dma((2,)), dma((2,)),
    ]
    vmem = pl.BlockSpec(memory_space=pltpu.VMEM)
    grad_frames, one, two = pl.pallas_call(
        functools.partial(kernel, sizes),
        out_shape=(
            jax.ShapeDtypeStruct((F, R, C, J), BF16),
            jax.ShapeDtypeStruct((2, 9, 3 * C, CC // 2), BF16),
            jax.ShapeDtypeStruct((2, 9, 3 * C, CC // 2), BF16),
        ),
        in_specs=[vmem] * 4,
        out_specs=(vmem,) * 3,
        scratch_shapes=scratch,
        compiler_params=pltpu.CompilerParams(
            collective_id=0, has_side_effects=True, vmem_limit_bytes=56 * 1024 * 1024
        ),
    )(frames, grad_out, taps_first(weight_one), taps_first(weight_two))

    def whole(grad):
        grad = grad.astype(F32)
        if T > 2:
            groups = [list(range(0, T, 2)), list(range(1, T, 2))]
            grad = lax.psum(grad, "tm", axis_index_groups=groups)
        grad = grad.reshape(2, 3, 3, 3, C, CC // 2).transpose(4, 1, 2, 3, 0, 5)
        return grad.reshape(C, 3, 3, 3, CC)

    return grad_frames, whole(one), whole(two)


def solution(mesh):
    sizes = (mesh.shape["tm"], mesh.shape["height"], mesh.shape["chan"])
    cells = P("tm", "height", "chan", None)
    filters = P("chan", None, None, None, None)
    return jax.shard_map(
        functools.partial(on_device, sizes),
        mesh=mesh,
        in_specs=(cells, cells, filters, filters),
        out_specs=(cells, filters, filters),
        check_vma=False,
    )
```

time: 318 us -> 77.8 us (0.24)
  the two profiles are of different devices: /device:TPU:0 before, /device:TPU:25 now
where the time goes in v1:
time: 77.8 us; the launch traced here: 77.6 us
  Pallas kernels  72.6 us (93%)
  other arithmetic  3.69 us (5%)
    pallas_call x1, Pallas kernels, on_device(): pl.pallas_call(functools.partial(kernel, sizes), out_shape=(jax.ShapeDtyp...  72.6 us
    reshape x1, other arithmetic, whole(): return grad.reshape(C, 3, 3, 3, CC)  3.69 us

profile of v1, /device:TPU:25, one launch (start us, length us, event | category | flops | bytes accessed | tf_op | source)
XLA Modules:
  0.0 77.6 jit_solution(15201726428103860408)
XLA Ops:
  0.6 72.6 %shard_map.67 = (bf16[2,4,64,128]{3,2,1,0:T(8,128)(2,1)}, bf16[2,9,192,128]{3,2,1,0:T(8,128)(2,1)}, bf16[2,9,192,128]{3,2,1,0:T(8,128)(2,1)}) custom-call(bf16[2,4,64,128]{3,2,1,0:T(8,128)(2,1)} %frames.1, bf16[2,4,64,128]{3,2,1,0:T(8,128)(2,1)} %gout.1, bf16[9,192,256]{2,1,0:T(8,128)(2,1)} %bitcast.22, bf16[9,192,256]{2,1,0:T(8,128)(2,1)} %bitcast.23), custom_call_target="tpu_custom_call" | custom-call | tf_op jit(solution)/shard_map/pallas_call | solution.py:406
  73.3 0.0 copy-start
  73.3 3.7 %copy_bitcast_fusion = (f32[64,3,3,3,256]{4,0,3,2,1:T(8,128)}, f32[64,3,3,3,256]{4,0,3,2,1:T(8,128)}) fusion(bf16[2,3,3,3,64,128]{5,4,3,2,1,0:T(8,128)(2,1)} %bitcast.24, bf16[2,3,3,3,64,128]{5,4,3,2,1,0:T(8,128)(2,1)} %bitcast.25), kind=kLoop, calls=%fused_computation | loop fusion | flops 884736 | bytes 5308416 | tf_op jit(solution)/shard_map/reshape | solution.py:427
  77.0 0.0 copy-done
  77.0 0.7 copy.14
Async XLA Ops:
  73.3 3.7 %copy-start = (bf16[2,4,64,128]{3,2,1,0:T(8,128)(2,1)S(1)}, bf16[2,4,64,128]{3,2,1,0:T(8,128)(2,1)}, u32[]{:S(2)}) copy-start(bf16[2,4,64,128]{3,2,1,0:T(8,128)(2,1)} %get-tuple-element.14) | copy-start | bytes 393220

commit v2 on v1

v2 whole, which is shorter than its diff:
```python
import functools

import jax
import jax.numpy as jnp
from jax import lax
from jax.experimental import pallas as pl
from jax.experimental.pallas import tpu as pltpu
from jax.sharding import PartitionSpec as P

BF16 = jnp.bfloat16
F32 = jnp.float32
MESH = pl.DeviceIdType.MESH
HALO = 5


def moved_cols(block, offset):
    lane = lax.broadcasted_iota(jnp.int32, block.shape, 1)
    cols = block.shape[1]
    if offset > 0:
        return jnp.where(lane == cols - 1, 0.0, pltpu.roll(block, cols - 1, 1))
    return jnp.where(lane == 0, 0.0, pltpu.roll(block, 1, 1))


def kernel(
    sizes,
    frames, gout, w1_in, w2_in,
    gf_out, g1_out, g2_out,
    w1, w2, x, g, gsh, gp, gpsh, w1t, w2t, pre, ga, gain, act, gf, gfin, via,
    town, tsend, trecv, hown, hsend, hrecv, fin,
    z_send, z_recv, zz_send, zz_recv, xh_send, xh_recv, gh_send, gh_recv,
    t_send, t_recv, h_send, h_recv, a_send, a_recv, p_send, p_recv, local,
):
    T, H, Z = sizes
    F, R, C, J = frames.shape
    CC = C * Z
    O = C
    slabs = F * R
    part = 3 * O // H
    FAR = 3 if Z == 4 else Z
    tm, h, z = lax.axis_index("tm"), lax.axis_index("height"), lax.axis_index("chan")
    pair = tm + 1 - 2 * lax.rem(tm, 2)
    parity = lax.rem(tm, 2)

    up, down = h > 0, h < H - 1
    has_prev, has_next = tm > 0, tm < T - 1

    def zpeer(d):
        return {"chan": lax.rem(z + d, Z)}

    def hpeer(d):
        return {"height": lax.rem(h + d, H)}

    both = jnp.logical_and

    loads = [
        pltpu.make_async_copy(w2_in, w2, local.at[0]),
        pltpu.make_async_copy(w1_in, w1, local.at[1]),
    ]
    for copy in loads:
        copy.start()

    barrier = pltpu.get_barrier_semaphore()
    for d in range(1, Z):
        pl.semaphore_signal(barrier, inc=1, device_id=zpeer(d), device_id_type=MESH)
    for d in range(1, H):
        pl.semaphore_signal(barrier, inc=1, device_id=hpeer(d), device_id_type=MESH)
    for cond_t, dt in ((has_prev, -1), (has_next, 1)):
        @pl.when(cond_t)
        def _(dt=dt):
            pl.semaphore_signal(barrier, inc=1, device_id={"tm": tm + dt}, device_id_type=MESH)
        for cond_h, dh in ((up, -1), (down, 1)):
            @pl.when(jnp.logical_and(cond_t, cond_h))
            def _(dt=dt, dh=dh):
                pl.semaphore_signal(
                    barrier, inc=1, device_id={"tm": tm + dt, "height": h + dh}, device_id_type=MESH
                )
    n_t = jnp.where(has_prev, 1, 0) + jnp.where(has_next, 1, 0)
    n_h = jnp.where(up, 1, 0) + jnp.where(down, 1, 0)
    pl.semaphore_wait(barrier, (Z - 1) + (H - 1) + n_t + n_t * n_h)

    pending = []

    def remote(src, dst, ssem, rsem, dev):
        return pltpu.make_async_remote_copy(
            src_ref=src, dst_ref=dst, send_sem=ssem, recv_sem=rsem, device_id=dev, device_id_type=MESH
        )

    def send(copy):
        copy.start()
        pending.append((None, copy))
        return copy

    def send_if(go, copy):
        pl.when(go)(copy.start)
        pending.append((go, copy))

    def halo_plan(ext, dt, chan_slice, ssems, rsems):
        o0, f0 = (F, 0) if dt > 0 else (0, F)
        to_t = has_next if dt > 0 else has_prev
        from_t = has_prev if dt > 0 else has_next

        def at(frame, row, rows):
            return ext.at[pl.ds(frame, F), pl.ds(row, rows), chan_slice, :]

        plan = [
            (to_t, from_t, at(o0, 1, R), at(f0, 1, R), {"tm": tm + dt}),
            (down, up, at(o0, R, 1), at(o0, 0, 1), {"height": h + 1}),
            (up, down, at(o0, 1, 1), at(o0, R + 1, 1), {"height": h - 1}),
            (
                both(to_t, down), both(from_t, up),
                at(o0, R, 1), at(f0, 0, 1), {"tm": tm + dt, "height": h + 1},
            ),
            (
                both(to_t, up), both(from_t, down),
                at(o0, 1, 1), at(f0, R + 1, 1), {"tm": tm + dt, "height": h - 1},
            ),
        ]
        return [
            (go, come, remote(src, dst, ssems.at[k], rsems.at[k], dev))
            for k, (go, come, src, dst, dev) in enumerate(plan)
        ]

    def depart(plan):
        for go, _, copy in plan:
            pl.when(go)(copy.start)

    def arrive(plan):
        for _, come, copy in plan:
            pl.when(come)(copy.wait_recv)

    def zero_edges(ext, dt):
        f0 = 0 if dt > 0 else F

        @pl.when(jnp.logical_not(has_prev if dt > 0 else has_next))
        def _():
            ext[f0 : f0 + F] = jnp.zeros((F,) + ext.shape[1:], ext.dtype)

        @pl.when(jnp.logical_not(up))
        def _():
            ext[:, 0] = jnp.zeros((2 * F,) + ext.shape[2:], ext.dtype)

        @pl.when(jnp.logical_not(down))
        def _():
            ext[:, R + 1] = jnp.zeros((2 * F,) + ext.shape[2:], ext.dtype)

    def chunk(index):
        return pl.ds(pl.multiple_of(index * C, C), C)

    mine = chunk(z)

    def near(p):
        return both(z != p, jnp.abs(z - p) < FAR)

    def gather(phase, block):
        for p in sorted(range(Z), key=lambda p: abs(2 * p - Z + 1)):
            send_if(near(p), remote(
                block(z), block(z), z_send.at[phase, p], z_recv.at[phase, z], {"chan": p}
            ))

    def nearest(k):
        low = z < Z // 2
        side = jnp.where(low, z, Z - 1 - z)
        other = jnp.where(k < side, k, k + 1)
        return jnp.where(low, other, Z - 1 - other)

    def gathered(phase, k, block):
        q = nearest(k)
        remote(
            block(q), block(q), z_send.at[phase, q], z_recv.at[phase, q], zpeer(1)
        ).wait_recv()
        if FAR < Z:
            for go, dz in (
                (both(both(q < z, z < Z - 1), z + 1 - q >= FAR), 1),
                (both(both(q > z, z > 0), q + 1 - z >= FAR), -1),
            ):
                send_if(go, remote(
                    block(q), block(q), zz_send.at[phase, k], z_recv.at[phase, q], {"chan": z + dz}
                ))
        return q

    ends = (0, Z - 1) if FAR < Z else ()

    def takes(p):
        return z == (1 if p == Z - 1 else Z - 2)

    def passed(phase, src, p):
        dz = 1 if p == Z - 1 else -1
        return remote(
            src.at[:, pl.ds(p * C, C), :], via.at[phase // 2],
            zz_send.at[phase, 0], zz_recv.at[phase], {"chan": lax.rem(z + dz + Z, Z)},
        )

    def direct(phase, src, dst, p):
        return remote(
            src.at[:, pl.ds(p * C, C), :], dst.at[z], z_send.at[phase, p], z_recv.at[phase, z], {"chan": p}
        )

    def scatter(phase, src, dst):
        for p in ends:
            send_if(z == Z - 1 - p, passed(phase, src, p))
        for p in range(Z):
            go = both(near(p), jnp.logical_not(takes(p))) if p in ends else near(p)
            pl.when(go)(direct(phase, src, dst, p).start)

    def scatter_rest(phase, src, dst):
        for p in ends:
            @pl.when(takes(p))
            def _(p=p):
                passed(phase, src, p).wait_recv()
                rows = slice(p * C, p * C + C)
                src[:, rows, :] = (
                    src[:, rows, :].astype(F32) + via[phase // 2].astype(F32)
                ).astype(BF16)
                direct(phase, src, dst, p).start()
        for p in range(Z):
            pending.append((near(p), direct(phase, src, dst, p)))

    def scattered(phase, src, dst):
        for q in range(Z):
            pl.when(near(q))(remote(
                src.at[:, pl.ds(0, C), :], dst.at[q], z_send.at[phase, q], z_recv.at[phase, q], zpeer(1)
            ).wait_recv)

    def summed(src, dst, s):
        total = src[s, mine, :].astype(F32)
        for q in range(Z):
            total += dst[q, s].astype(F32)
        return total

    def x_block(q):
        return x.at[pl.ds(F, F), pl.ds(1, R), chunk(q), :]

    def act_block(q):
        return act.at[:, chunk(q), :]

    def x_halo(q):
        return halo_plan(x, 1, chunk(q), xh_send.at[q], xh_recv.at[q])

    x[F : 2 * F, 1 : R + 1, mine, :] = frames[...]
    gather(0, x_block)
    g[0:F, 1 : R + 1] = gout[...]
    g_plan = halo_plan(g, -1, pl.ds(0, C), gh_send.at[0], gh_recv.at[0])
    depart(g_plan)
    depart(x_halo(z))
    zero_edges(g, -1)
    zero_edges(gp, -1)
    zero_edges(x, 1)
    for dst in (gain, gfin):
        for q in range(Z):
            @pl.when(jnp.logical_not(near(q)))
            def _(dst=dst, q=q):
                dst[q] = jnp.zeros(dst.shape[1:], dst.dtype)

    loads[0].wait()

    @pl.loop(0, 9)
    def _(ab):
        w2t[ab] = w2[ab].T

    def spread(src, dst, t, i):
        wide = src[t, i].astype(F32)
        dst[t, i, 0:O] = moved_cols(wide, 1).astype(BF16)
        dst[t, i, O : 2 * O] = src[t, i]
        dst[t, i, 2 * O : 3 * O] = moved_cols(wide, -1).astype(BF16)

    def back(source, weight, out):
        @pl.loop(0, slabs // 2)
        def _(s):
            t, i = s // (R // 2), 2 * lax.rem(s, R // 2)
            total = jnp.zeros((CC, 2 * J), F32)
            for a in range(3):
                for b in range(3):
                    window = jnp.concatenate(
                        [source[t + 2 - a, i + 2 - b], source[t + 2 - a, i + 3 - b]], 1
                    )
                    total += jnp.dot(weight[a * 3 + b], window, preferred_element_type=F32)
            out[2 * s] = total[:, :J].astype(BF16)
            out[2 * s + 1] = total[:, J:].astype(BF16)

    arrive(g_plan)

    @pl.loop(0, 2 * F * (R + 2))
    def _(s):
        spread(g, gsh, s // (R + 2), lax.rem(s, R + 2))

    back(gsh, w2t, ga)
    scatter(1, ga, gain)
    loads[1].wait()

    for k in range(Z - 1):
        depart(x_halo(gathered(0, k, x_block)))
    scatter_rest(1, ga, gain)

    @pl.loop(0, 9)
    def _(ab):
        w1t[ab] = w1[ab].T

    for q in range(Z):
        arrive(x_halo(q))

    @pl.loop(0, slabs // 2)
    def _(s):
        t, i = s // (R // 2), 2 * lax.rem(s, R // 2)
        total = jnp.zeros((3 * O, 2 * J), F32)
        for a in range(3):
            for b in range(3):
                window = jnp.concatenate([x[t + a, i + b], x[t + a, i + b + 1]], 1)
                total += jnp.dot(w1[a * 3 + b], window, preferred_element_type=F32)
        for half in range(2):
            cols = total[:, half * J : (half + 1) * J]
            value = moved_cols(cols[0:O], -1) + cols[O : 2 * O] + moved_cols(cols[2 * O :], 1)
            pre[2 * s + half] = value
            act[2 * s + half, mine, :] = (value * jax.nn.sigmoid(value)).astype(BF16)

    scattered(1, ga, gain)

    @pl.loop(0, slabs)
    def _(s):
        t, i = s // R, lax.rem(s, R)
        total = summed(ga, gain, s)
        value = pre[s]
        sig = jax.nn.sigmoid(value)
        gp[t, i + 1] = (total * sig * (1.0 + value * (1.0 - sig))).astype(BF16)

    gp_plan = halo_plan(gp, -1, pl.ds(0, C), gh_send.at[1], gh_recv.at[1])
    depart(gp_plan)
    gather(2, act_block)

    @pl.loop(0, slabs)
    def _(s):
        spread(gp, gpsh, s // R, lax.rem(s, R) + 1)

    nt = (((1,), (1,)), ((), ()))

    def row_of(source, t0, i0):
        return jnp.concatenate([source[t0 + s // R, i0 + s % R] for s in range(slabs)], 1)

    my_rows = pl.ds(pl.multiple_of(h * part, part), part)

    def taps(a):
        return pl.ds(3 * a, 3)

    def to_pair(f, a, left_of, right_of):
        @pl.loop(0, 3)
        def _(b):
            value = lax.dot_general(left_of(a, b), right_of(a, b), nt, preferred_element_type=F32)
            left, right = value[:, :J], value[:, J:]
            town[f, 3 * a + b] = jnp.where(parity == 0, left, right)
            tsend[f, 3 * a + b] = jnp.where(parity == 0, right, left).astype(BF16)

        return send(remote(
            tsend.at[f, taps(a)], trecv.at[f, taps(a)], t_send.at[f, a], t_recv.at[f, a], {"tm": pair}
        ))

    def to_rows(f, a, copy):
        copy.wait_recv()

        @pl.loop(3 * a, 3 * a + 3)
        def _(ab):
            total = town[f, ab] + trecv[f, ab].astype(F32)
            hown[f, ab] = total
            hsend[f, ab] = total.astype(BF16)

        return [
            send(remote(
                hsend.at[f, taps(a), pl.ds(pl.multiple_of(lax.rem(h + d, H) * part, part), part), :],
                hrecv.at[f, d - 1, taps(a)],
                h_send.at[f, a, d - 1], h_recv.at[f, a, d - 1], hpeer(d),
            ))
            for d in range(1, H)
        ]

    def piece(f, a, row):
        return fin.at[f, parity, taps(a), pl.ds(pl.multiple_of(row * part, part), part), :]

    def relay(f, a, d):
        block = piece(f, a, lax.rem(h - d + H, H))
        return send(remote(block, block, p_send.at[f, a, d], p_recv.at[f, a, d], {"tm": pair}))

    def from_rows(f, a, copies):
        for copy in copies:
            copy.wait_recv()

        @pl.loop(3 * a, 3 * a + 3)
        def _(ab):
            total = hown[f, ab, my_rows, :]
            for d in range(1, H):
                total += hrecv[f, d - 1, ab].astype(F32)
            fin[f, parity, ab, my_rows, :] = total.astype(BF16)

        block = piece(f, a, h)
        copies = [
            send(remote(block, block, a_send.at[f, a, d - 1], a_recv.at[f, a, d - 1], hpeer(d)))
            for d in range(1, H)
        ]
        return copies, [relay(f, a, 0)]

    def to_other(f, a, state):
        copies, relays = state
        for d in range(1, H):
            copies[d - 1].wait_recv()
            relays.append(relay(f, a, d))
        return relays

    def first_left(a, b):
        return row_of(gpsh, 0, 1)

    def first_right(a, b):
        return row_of(x, a, b)

    def second_left(a, b):
        return row_of(gsh, 2 - a, 2 - b)

    def second_right(a, b):
        return jnp.concatenate([act[s] for s in range(slabs)], 1)

    one = [to_pair(0, a, first_left, first_right) for a in range(3)]
    one = [to_rows(0, a, one[a]) for a in range(3)]

    arrive(gp_plan)

    @pl.loop(0, F * (R + 2))
    def _(s):
        spread(gp, gpsh, F + s // (R + 2), lax.rem(s, R + 2))

    for t in range(F):
        for i in (0, R + 1):
            spread(gp, gpsh, t, i)
    back(gpsh, w1t, gf)

    for k in range(Z - 1):
        gathered(2, k, act_block)
    scatter(3, gf, gfin)

    two = [to_pair(1, a, second_left, second_right) for a in range(3)]
    one = [from_rows(0, a, one[a]) for a in range(3)]
    two = [to_rows(1, a, two[a]) for a in range(3)]
    scatter_rest(3, gf, gfin)
    one = [to_other(0, a, one[a]) for a in range(3)]
    two = [from_rows(1, a, two[a]) for a in range(3)]

    for relays in one:
        for copy in relays:
            copy.wait_recv()
    stores = [pltpu.make_async_copy(fin.at[0], g1_out, local.at[2])]
    stores[0].start()
    two = [to_other(1, a, two[a]) for a in range(3)]
    scattered(3, gf, gfin)

    @pl.loop(0, slabs)
    def _(s):
        gf_out[s // R, lax.rem(s, R)] = summed(gf, gfin, s).astype(BF16)

    for relays in two:
        for copy in relays:
            copy.wait_recv()
    stores.append(pltpu.make_async_copy(fin.at[1], g2_out, local.at[3]))
    stores[1].start()

    for go, copy in pending:
        if go is None:
            copy.wait_send()
        else:
            pl.when(go)(copy.wait_send)
    for plan in [g_plan, gp_plan] + [x_halo(q) for q in range(Z)]:
        for go, _, copy in plan:
            pl.when(go)(copy.wait_send)
    for copy in stores:
        copy.wait()


def on_device(sizes, frames, grad_out, weight_one, weight_two):
    T, H, Z = sizes
    F, R, C, J = frames.shape
    CC, slabs, part = C * Z, F * R, 3 * C // H

    def taps_first(weight):
        return weight.transpose(1, 2, 3, 0, 4).reshape(9, 3 * C, CC)

    dma = pltpu.SemaphoreType.DMA
    ext = (2 * F, R + 2)
    scratch = [
        pltpu.VMEM((9, 3 * C, CC), BF16),
        pltpu.VMEM((9, 3 * C, CC), BF16),
        pltpu.VMEM(ext + (CC, J), BF16),
        pltpu.VMEM(ext + (C, J), BF16),
        pltpu.VMEM(ext + (3 * C, J), BF16),
        pltpu.VMEM(ext + (C, J), BF16),
        pltpu.VMEM(ext + (3 * C, J), BF16),
        pltpu.VMEM((9, CC, 3 * C), BF16),
        pltpu.VMEM((9, CC, 3 * C), BF16),
        pltpu.VMEM((slabs, C, J), F32),
        pltpu.VMEM((slabs, CC, J), BF16),
        pltpu.VMEM((Z, slabs, C, J), BF16),
        pltpu.VMEM((slabs, CC, J), BF16),
        pltpu.VMEM((slabs, CC, J), BF16),
        pltpu.VMEM((Z, slabs, C, J), BF16),
        pltpu.VMEM((2, slabs, C, J), BF16),
        pltpu.VMEM((2, 9, 3 * C, CC // 2), F32),
        pltpu.VMEM((2, 9, 3 * C, CC // 2), BF16),
        pltpu.VMEM((2, 9, 3 * C, CC // 2), BF16),
        pltpu.VMEM((2, 9, 3 * C, CC // 2), F32),
        pltpu.VMEM((2, 9, 3 * C, CC // 2), BF16),
        pltpu.VMEM((2, H - 1, 9, part, CC // 2), BF16),
        pltpu.VMEM((2, 2, 9, 3 * C, CC // 2), BF16),
        dma((4, Z)), dma((4, Z)), dma((4, Z)), dma((4,)),
        dma((Z, HALO)), dma((Z, HALO)), dma((2, HALO)), dma((2, HALO)),
        dma((2, 3)), dma((2, 3)), dma((2, 3, H - 1)), dma((2, 3, H - 1)),
        dma((2, 3, H - 1)), dma((2, 3, H - 1)), dma((2, 3, H)), dma((2, 3, H)), dma((4,)),
    ]
    vmem = pl.BlockSpec(memory_space=pltpu.VMEM)
    hbm = pl.BlockSpec(memory_space=pl.ANY)
    grad_frames, one, two = pl.pallas_call(
        functools.partial(kernel, sizes),
        out_shape=(
            jax.ShapeDtypeStruct((F, R, C, J), BF16),
            jax.ShapeDtypeStruct((2, 9, 3 * C, CC // 2), BF16),
            jax.ShapeDtypeStruct((2, 9, 3 * C, CC // 2), BF16),
        ),
        in_specs=[vmem, vmem, hbm, hbm],
        out_specs=(vmem, hbm, hbm),
        scratch_shapes=scratch,
        compiler_params=pltpu.CompilerParams(
            collective_id=0, has_side_effects=True, vmem_limit_bytes=56 * 1024 * 1024
        ),
    )(frames, grad_out, taps_first(weight_one), taps_first(weight_two))

    def whole(grad):
        grad = grad.astype(F32)
        if T > 2:
            groups = [list(range(0, T, 2)), list(range(1, T, 2))]
            grad = lax.psum(grad, "tm", axis_index_groups=groups)
        grad = grad.reshape(2, 3, 3, 3, C, CC // 2).transpose(4, 1, 2, 3, 0, 5)
        return grad.reshape(C, 3, 3, 3, CC)

    return grad_frames, whole(one), whole(two)


def solution(mesh):
    sizes = (mesh.shape["tm"], mesh.shape["height"], mesh.shape["chan"])
    cells = P("tm", "height", "chan", None)
    filters = P("chan", None, None, None, None)
    return jax.shard_map(
        functools.partial(on_device, sizes),
        mesh=mesh,
        in_specs=(cells, cells, filters, filters),
        out_specs=(cells, filters, filters),
        check_vma=False,
    )
```

time: 77.8 us -> 69 us (0.89)
  the two profiles are of different devices: /device:TPU:25 before, /device:TPU:0 now
where the time goes in v2:
time: 69 us; the launch traced here: 67.8 us
  Pallas kernels  62.8 us (91%)
  other arithmetic  3.69 us (5%)
    pallas_call x1, Pallas kernels, on_device(): pl.pallas_call(functools.partial(kernel, sizes), out_shape=(jax.ShapeDtyp...  62.8 us
    reshape x1, other arithmetic, whole(): return grad.reshape(C, 3, 3, 3, CC)  3.69 us

profile of v2, /device:TPU:0, one launch (start us, length us, event | category | flops | bytes accessed | tf_op | source)
XLA Modules:
  0.0 67.8 jit_solution(12739835832076193458)
XLA Ops:
  0.6 62.8 %shard_map.67 = (bf16[2,4,64,128]{3,2,1,0:T(8,128)(2,1)}, bf16[2,9,192,128]{3,2,1,0:T(8,128)(2,1)}, bf16[2,9,192,128]{3,2,1,0:T(8,128)(2,1)}) custom-call(bf16[2,4,64,128]{3,2,1,0:T(8,128)(2,1)} %frames.1, bf16[2,4,64,128]{3,2,1,0:T(8,128)(2,1)} %gout.1, bf16[9,192,256]{2,1,0:T(8,128)(2,1)} %bitcast.22, bf16[9,192,256]{2,1,0:T(8,128)(2,1)} %bitcast.23), custom_call_target="tpu_custom_call" | custom-call | tf_op jit(solution)/shard_map/pallas_call | solution.py:513
  63.5 0.0 copy-start
  63.5 3.7 %copy_bitcast_fusion = (f32[64,3,3,3,256]{4,0,3,2,1:T(8,128)}, f32[64,3,3,3,256]{4,0,3,2,1:T(8,128)}) fusion(bf16[2,3,3,3,64,128]{5,4,3,2,1,0:T(8,128)(2,1)} %bitcast.24, bf16[2,3,3,3,64,128]{5,4,3,2,1,0:T(8,128)(2,1)} %bitcast.25), kind=kLoop, calls=%fused_computation | loop fusion | flops 884736 | bytes 5308416 | tf_op jit(solution)/shard_map/reshape | solution.py:534
  67.2 0.0 copy-done
  67.2 0.7 copy.14
Async XLA Ops:
  63.5 3.7 %copy-start = (bf16[2,4,64,128]{3,2,1,0:T(8,128)(2,1)S(1)}, bf16[2,4,64,128]{3,2,1,0:T(8,128)(2,1)}, u32[]{:S(2)}) copy-start(bf16[2,4,64,128]{3,2,1,0:T(8,128)(2,1)} %get-tuple-element.14) | copy-start | bytes 393220

commit v3 on v2

--- a/solution.py
+++ b/solution.py
@@ -31,7 +31,7 @@
     t_send, t_recv, h_send, h_recv, a_send, a_recv, p_send, p_recv, local,
 ):
     T, H, Z = sizes
-    F, R, C, J = frames.shape
+    F, R, C, J = gf_out.shape
     CC = C * Z
     O = C
     slabs = F * R
@@ -55,9 +55,15 @@
     loads = [
         pltpu.make_async_copy(w2_in, w2, local.at[0]),
         pltpu.make_async_copy(w1_in, w1, local.at[1]),
+        pltpu.make_async_copy(
+            frames,
+            x.at[pl.ds(F, F), pl.ds(1, R), pl.ds(pl.multiple_of(z * C, C), C), :],
+            local.at[4],
+        ),
+        pltpu.make_async_copy(gout, g.at[pl.ds(0, F), pl.ds(1, R)], local.at[5]),
     ]
-    for copy in loads:
-        copy.start()
+    for k in (2, 3, 0, 1):
+        loads[k].start()
 
     barrier = pltpu.get_barrier_semaphore()
     for d in range(1, Z):
@@ -74,6 +80,33 @@
                 pl.semaphore_signal(
                     barrier, inc=1, device_id={"tm": tm + dt, "height": h + dh}, device_id_type=MESH
                 )
+    def near(p):
+        return both(z != p, jnp.abs(z - p) < FAR)
+
+    def zero_edges(ext, dt):
+        f0 = 0 if dt > 0 else F
+
+        @pl.when(jnp.logical_not(has_prev if dt > 0 else has_next))
+        def _():
+            ext[f0 : f0 + F] = jnp.zeros((F,) + ext.shape[1:], ext.dtype)
+
+        @pl.when(jnp.logical_not(up))
+        def _():
+            ext[:, 0] = jnp.zeros((2 * F,) + ext.shape[2:], ext.dtype)
+
+        @pl.when(jnp.logical_not(down))
+        def _():
+            ext[:, R + 1] = jnp.zeros((2 * F,) + ext.shape[2:], ext.dtype)
+
+    zero_edges(g, -1)
+    zero_edges(gp, -1)
+    zero_edges(x, 1)
+    for dst in (gain, gfin):
+        for q in range(Z):
+            @pl.when(jnp.logical_not(near(q)))
+            def _(dst=dst, q=q):
+                dst[q] = jnp.zeros(dst.shape[1:], dst.dtype)
+
     n_t = jnp.where(has_prev, 1, 0) + jnp.where(has_next, 1, 0)
     n_h = jnp.where(up, 1, 0) + jnp.where(down, 1, 0)
     pl.semaphore_wait(barrier, (Z - 1) + (H - 1) + n_t + n_t * n_h)
@@ -128,28 +161,10 @@
         for _, come, copy in plan:
             pl.when(come)(copy.wait_recv)
 
-    def zero_edges(ext, dt):
-        f0 = 0 if dt > 0 else F
-
-        @pl.when(jnp.logical_not(has_prev if dt > 0 else has_next))
-        def _():
-            ext[f0 : f0 + F] = jnp.zeros((F,) + ext.shape[1:], ext.dtype)
-
-        @pl.when(jnp.logical_not(up))
-        def _():
-            ext[:, 0] = jnp.zeros((2 * F,) + ext.shape[2:], ext.dtype)
-
-        @pl.when(jnp.logical_not(down))
-        def _():
-            ext[:, R + 1] = jnp.zeros((2 * F,) + ext.shape[2:], ext.dtype)
-
     def chunk(index):
         return pl.ds(pl.multiple_of(index * C, C), C)
 
     mine = chunk(z)
-
-    def near(p):
-        return both(z != p, jnp.abs(z - p) < FAR)
 
     def gather(phase, block):
         for p in sorted(range(Z), key=lambda p: abs(2 * p - Z + 1)):
@@ -236,26 +251,21 @@
     def x_halo(q):
         return halo_plan(x, 1, chunk(q), xh_send.at[q], xh_recv.at[q])
 
-    x[F : 2 * F, 1 : R + 1, mine, :] = frames[...]
+    loads[2].wait()
     gather(0, x_block)
-    g[0:F, 1 : R + 1] = gout[...]
+    loads[3].wait()
     g_plan = halo_plan(g, -1, pl.ds(0, C), gh_send.at[0], gh_recv.at[0])
     depart(g_plan)
     depart(x_halo(z))
-    zero_edges(g, -1)
-    zero_edges(gp, -1)
-    zero_edges(x, 1)
-    for dst in (gain, gfin):
-        for q in range(Z):
-            @pl.when(jnp.logical_not(near(q)))
-            def _(dst=dst, q=q):
-                dst[q] = jnp.zeros(dst.shape[1:], dst.dtype)
+    def turned(weight, out):
+        flat = weight[...].reshape(27 * O, CC)
+        for k in range(0, 27 * O, 2 * J):
+            end = min(k + 2 * J, 27 * O)
+            out[:, k:end] = flat[k:end].T
 
     loads[0].wait()
 
-    @pl.loop(0, 9)
-    def _(ab):
-        w2t[ab] = w2[ab].T
+    turned(w2, w2t)
 
     def spread(src, dst, t, i):
         wide = src[t, i].astype(F32)
@@ -267,19 +277,18 @@
         @pl.loop(0, slabs // 2)
         def _(s):
             t, i = s // (R // 2), 2 * lax.rem(s, R // 2)
-            total = jnp.zeros((CC, 2 * J), F32)
-            for a in range(3):
-                for b in range(3):
-                    window = jnp.concatenate(
-                        [source[t + 2 - a, i + 2 - b], source[t + 2 - a, i + 3 - b]], 1
-                    )
-                    total += jnp.dot(weight[a * 3 + b], window, preferred_element_type=F32)
+            windows = [
+                jnp.concatenate([source[t + 2 - a, i + 2 - b], source[t + 2 - a, i + 3 - b]], 1)
+                for a in range(3)
+                for b in range(3)
+            ]
+            total = jnp.dot(weight[...], jnp.concatenate(windows, 0), preferred_element_type=F32)
             out[2 * s] = total[:, :J].astype(BF16)
             out[2 * s + 1] = total[:, J:].astype(BF16)
 
     arrive(g_plan)
 
-    @pl.loop(0, 2 * F * (R + 2))
+    @pl.loop(0, 2 * F * (R + 2), unroll=4)
     def _(s):
         spread(g, gsh, s // (R + 2), lax.rem(s, R + 2))
 
@@ -291,9 +300,7 @@
         depart(x_halo(gathered(0, k, x_block)))
     scatter_rest(1, ga, gain)
 
-    @pl.loop(0, 9)
-    def _(ab):
-        w1t[ab] = w1[ab].T
+    turned(w1, w1t)
 
     for q in range(Z):
         arrive(x_halo(q))
@@ -301,11 +308,13 @@
     @pl.loop(0, slabs // 2)
     def _(s):
         t, i = s // (R // 2), 2 * lax.rem(s, R // 2)
-        total = jnp.zeros((3 * O, 2 * J), F32)
-        for a in range(3):
-            for b in range(3):
-                window = jnp.concatenate([x[t + a, i + b], x[t + a, i + b + 1]], 1)
-                total += jnp.dot(w1[a * 3 + b], window, preferred_element_type=F32)
+        windows = [
+            jnp.concatenate([x[t + a, i + b], x[t + a, i + b + 1]], 1)
+            for a in range(3)
+            for b in range(3)
+        ]
+        taps_of = jnp.concatenate([w1[ab] for ab in range(9)], 1)
+        total = jnp.dot(taps_of, jnp.concatenate(windows, 0), preferred_element_type=F32)
         for half in range(2):
             cols = total[:, half * J : (half + 1) * J]
             value = moved_cols(cols[0:O], -1) + cols[O : 2 * O] + moved_cols(cols[2 * O :], 1)
@@ -313,8 +322,9 @@
             act[2 * s + half, mine, :] = (value * jax.nn.sigmoid(value)).astype(BF16)
 
     scattered(1, ga, gain)
-
-    @pl.loop(0, slabs)
+    gather(2, act_block)
+
+    @pl.loop(0, slabs, unroll=4)
     def _(s):
         t, i = s // R, lax.rem(s, R)
         total = summed(ga, gain, s)
@@ -324,9 +334,8 @@
 
     gp_plan = halo_plan(gp, -1, pl.ds(0, C), gh_send.at[1], gh_recv.at[1])
     depart(gp_plan)
-    gather(2, act_block)
-
-    @pl.loop(0, slabs)
+
+    @pl.loop(0, slabs, unroll=4)
     def _(s):
         spread(gp, gpsh, s // R, lax.rem(s, R) + 1)
 
@@ -355,7 +364,7 @@
     def to_rows(f, a, copy):
         copy.wait_recv()
 
-        @pl.loop(3 * a, 3 * a + 3)
+        @pl.loop(3 * a, 3 * a + 3, unroll=3)
         def _(ab):
             total = town[f, ab] + trecv[f, ab].astype(F32)
             hown[f, ab] = total
@@ -381,7 +390,7 @@
         for copy in copies:
             copy.wait_recv()
 
-        @pl.loop(3 * a, 3 * a + 3)
+        @pl.loop(3 * a, 3 * a + 3, unroll=3)
         def _(ab):
             total = hown[f, ab, my_rows, :]
             for d in range(1, H):
@@ -419,7 +428,7 @@
 
     arrive(gp_plan)
 
-    @pl.loop(0, F * (R + 2))
+    @pl.loop(0, F * (R + 2), unroll=4)
     def _(s):
         spread(gp, gpsh, F + s // (R + 2), lax.rem(s, R + 2))
 
@@ -447,7 +456,7 @@
     two = [to_other(1, a, two[a]) for a in range(3)]
     scattered(3, gf, gfin)
 
-    @pl.loop(0, slabs)
+    @pl.loop(0, slabs, unroll=4)
     def _(s):
         gf_out[s // R, lax.rem(s, R)] = summed(gf, gfin, s).astype(BF16)
 
@@ -487,8 +496,8 @@
         pltpu.VMEM(ext + (3 * C, J), BF16),
         pltpu.VMEM(ext + (C, J), BF16),
         pltpu.VMEM(ext + (3 * C, J), BF16),
-        pltpu.VMEM((9, CC, 3 * C), BF16),
-        pltpu.VMEM((9, CC, 3 * C), BF16),
+        pltpu.VMEM((CC, 27 * C), BF16),
+        pltpu.VMEM((CC, 27 * C), BF16),
         pltpu.VMEM((slabs, C, J), F32),
         pltpu.VMEM((slabs, CC, J), BF16),
         pltpu.VMEM((Z, slabs, C, J), BF16),
@@ -506,7 +515,7 @@
         dma((4, Z)), dma((4, Z)), dma((4, Z)), dma((4,)),
         dma((Z, HALO)), dma((Z, HALO)), dma((2, HALO)), dma((2, HALO)),
         dma((2, 3)), dma((2, 3)), dma((2, 3, H - 1)), dma((2, 3, H - 1)),
-        dma((2, 3, H - 1)), dma((2, 3, H - 1)), dma((2, 3, H)), dma((2, 3, H)), dma((4,)),
+        dma((2, 3, H - 1)), dma((2, 3, H - 1)), dma((2, 3, H)), dma((2, 3, H)), dma((6,)),
     ]
     vmem = pl.BlockSpec(memory_space=pltpu.VMEM)
     hbm = pl.BlockSpec(memory_space=pl.ANY)
@@ -517,7 +526,7 @@
             jax.ShapeDtypeStruct((2, 9, 3 * C, CC // 2), BF16),
             jax.ShapeDtypeStruct((2, 9, 3 * C, CC // 2), BF16),
         ),
-        in_specs=[vmem, vmem, hbm, hbm],
+        in_specs=[hbm] * 4,
         out_specs=(vmem, hbm, hbm),
         scratch_shapes=scratch,
         compiler_params=pltpu.CompilerParams(
@@ -525,13 +534,30 @@
         ),
     )(frames, grad_out, taps_first(weight_one), taps_first(weight_two))
 
+    def widened(cells_in, one_in, two_in, cells_out, one_out, two_out):
+        cells_out[...] = cells_in[...]
+        for narrow, wide in ((one_in, one_out), (two_in, two_out)):
+            for half in range(2):
+                wide[:, :, half * CC // 2 : (half + 1) * CC // 2] = narrow[half].astype(F32)
+
+    cells = pl.BlockSpec((F, R, C, J), lambda a: (0, 0, 0, 0))
+    narrow = pl.BlockSpec((2, 3, 3 * C, CC // 2), lambda a: (0, a, 0, 0))
+    wide = pl.BlockSpec((3, 3 * C, CC), lambda a: (a, 0, 0))
+    filters = jax.ShapeDtypeStruct((9, 3 * C, CC), F32)
+    grad_frames, one, two = pl.pallas_call(
+        widened,
+        grid=(3,),
+        out_shape=(jax.ShapeDtypeStruct((F, R, C, J), BF16), filters, filters),
+        in_specs=[cells, narrow, narrow],
+        out_specs=(cells, wide, wide),
+        compiler_params=pltpu.CompilerParams(vmem_limit_bytes=56 * 1024 * 1024),
+    )(grad_frames, one, two)
+
     def whole(grad):
-        grad = grad.astype(F32)
         if T > 2:
             groups = [list(range(0, T, 2)), list(range(1, T, 2))]
             grad = lax.psum(grad, "tm", axis_index_groups=groups)
-        grad = grad.reshape(2, 3, 3, 3, C, CC // 2).transpose(4, 1, 2, 3, 0, 5)
-        return grad.reshape(C, 3, 3, 3, CC)
+        return grad.reshape(3, 3, 3, C, CC).transpose(3, 0, 1, 2, 4)
 
     return grad_frames, whole(one), whole(two)
 

time: 69 us -> 65.5 us (0.949)
  other arithmetic: 3.69 us -> 0 us
  Pallas kernels: 62.8 us -> 64 us
    pallas_call x0 -> x1, Pallas kernels: none -> 3.85 us  [on_device(): pl.pallas_call(widened, grid=(3,), out_shape=(jax.ShapeDtypeStruct((F, R,...]
    reshape x1 -> x0, other arithmetic: 3.69 us -> none  [whole(): return grad.reshape(C, 3, 3, 3, CC)]
    pallas_call x1, Pallas kernels: 62.8 us -> 60.2 us  [on_device(): pl.pallas_call(functools.partial(kernel, sizes), out_shape=(jax.ShapeDtyp...]
where the time goes in v3:
time: 65.5 us; the launch traced here: 64.7 us
  Pallas kernels  64 us (98%)
    pallas_call x1, Pallas kernels, on_device(): pl.pallas_call(functools.partial(kernel, sizes), out_shape=(jax.ShapeDtyp...  60.2 us
    pallas_call x1, Pallas kernels, on_device(): pl.pallas_call(widened, grid=(3,), out_shape=(jax.ShapeDtypeStruct((F, R,...  3.85 us

profile of v3, /device:TPU:0, one launch (start us, length us, event | category | flops | bytes accessed | tf_op | source)
XLA Modules:
  0.0 64.7 jit_solution(5322597181159670762)
XLA Ops:
  0.6 60.2 %shard_map.67 = (bf16[2,4,64,128]{3,2,1,0:T(8,128)(2,1)}, bf16[2,9,192,128]{3,2,1,0:T(8,128)(2,1)}, bf16[2,9,192,128]{3,2,1,0:T(8,128)(2,1)}) custom-call(bf16[2,4,64,128]{3,2,1,0:T(8,128)(2,1)} %frames.1, bf16[2,4,64,128]{3,2,1,0:T(8,128)(2,1)} %gout.1, bf16[9,192,256]{2,1,0:T(8,128)(2,1)} %bitcast.12, bf16[9,192,256]{2,1,0:T(8,128)(2,1)} %bitcast.13), custom_call_target="tpu_custom_call" | custom-call | tf_op jit(solution)/shard_map/pallas_call | solution.py:522
  60.8 3.9 %shard_map.68 = (bf16[2,4,64,128]{3,2,1,0:T(8,128)(2,1)}, f32[9,192,256]{2,1,0:T(8,128)}, f32[9,192,256]{2,1,0:T(8,128)}) custom-call(bf16[2,4,64,128]{3,2,1,0:T(8,128)(2,1)} %get-tuple-element.9.cells_in, bf16[2,9,192,128]{3,2,1,0:T(8,128)(2,1)} %get-tuple-element.10.one_in, bf16[2,9,192,128]{3,2,1,0:T(8,128)(2,1)} %get-tuple-element.11.two_in), custom_call_target="tpu_custom_call" | custom-call | tf_op jit(solution)/shard_map/pallas_call | solution.py:547

commit v4 on v3

--- a/solution.py
+++ b/solution.py
@@ -25,7 +25,7 @@
     sizes,
     frames, gout, w1_in, w2_in,
     gf_out, g1_out, g2_out,
-    w1, w2, x, g, gsh, gp, gpsh, w1t, w2t, pre, ga, gain, act, gf, gfin, via,
+    w1, w2, w1c, raw, x, g, gsh, gp, gpsh, w1t, w2t, pre, ga, gain, act, gf, gfin, via,
     town, tsend, trecv, hown, hsend, hrecv, fin,
     z_send, z_recv, zz_send, zz_recv, xh_send, xh_recv, gh_send, gh_recv,
     t_send, t_recv, h_send, h_recv, a_send, a_recv, p_send, p_recv, local,
@@ -296,30 +296,44 @@
     scatter(1, ga, gain)
     loads[1].wait()
 
+    for q in range(Z):
+        w1c[q] = jnp.concatenate([w1[ab][:, q * C : (q + 1) * C] for ab in range(9)], 1)
+
+    def forward(q, first=False, last=False):
+        channels = chunk(q)
+
+        @pl.loop(0, slabs // 2)
+        def _(s):
+            t, i = s // (R // 2), 2 * lax.rem(s, R // 2)
+            windows = [
+                jnp.concatenate([x[t + a, i + b, channels, :], x[t + a, i + b + 1, channels, :]], 1)
+                for a in range(3)
+                for b in range(3)
+            ]
+            total = jnp.dot(w1c[q], jnp.concatenate(windows, 0), preferred_element_type=F32)
+            if not first:
+                total += raw[s]
+            if not last:
+                raw[s] = total
+                return
+            for half in range(2):
+                cols = total[:, half * J : (half + 1) * J]
+                value = moved_cols(cols[0:O], -1) + cols[O : 2 * O] + moved_cols(cols[2 * O :], 1)
+                pre[2 * s + half] = value
+                act[2 * s + half, mine, :] = (value * jax.nn.sigmoid(value)).astype(BF16)
+
+    before = z
     for k in range(Z - 1):
-        depart(x_halo(gathered(0, k, x_block)))
-    scatter_rest(1, ga, gain)
-
+        q = gathered(0, k, x_block)
+        depart(x_halo(q))
+        if k == Z - 2:
+            scatter_rest(1, ga, gain)
+        arrive(x_halo(before))
+        forward(before, first=k == 0)
+        before = q
     turned(w1, w1t)
-
-    for q in range(Z):
-        arrive(x_halo(q))
-
-    @pl.loop(0, slabs // 2)
-    def _(s):
-        t, i = s // (R // 2), 2 * lax.rem(s, R // 2)
-        windows = [
-            jnp.concatenate([x[t + a, i + b], x[t + a, i + b + 1]], 1)
-            for a in range(3)
-            for b in range(3)
-        ]
-        taps_of = jnp.concatenate([w1[ab] for ab in range(9)], 1)
-        total = jnp.dot(taps_of, jnp.concatenate(windows, 0), preferred_element_type=F32)
-        for half in range(2):
-            cols = total[:, half * J : (half + 1) * J]
-            value = moved_cols(cols[0:O], -1) + cols[O : 2 * O] + moved_cols(cols[2 * O :], 1)
-            pre[2 * s + half] = value
-            act[2 * s + half, mine, :] = (value * jax.nn.sigmoid(value)).astype(BF16)
+    arrive(x_halo(before))
+    forward(before, last=True)
 
     scattered(1, ga, gain)
     gather(2, act_block)
@@ -436,23 +450,29 @@
         for i in (0, R + 1):
             spread(gp, gpsh, t, i)
     back(gpsh, w1t, gf)
+    one = [from_rows(0, a, one[a]) for a in range(3)]
 
     for k in range(Z - 1):
         gathered(2, k, act_block)
     scatter(3, gf, gfin)
 
     two = [to_pair(1, a, second_left, second_right) for a in range(3)]
-    one = [from_rows(0, a, one[a]) for a in range(3)]
     two = [to_rows(1, a, two[a]) for a in range(3)]
     scatter_rest(3, gf, gfin)
     one = [to_other(0, a, one[a]) for a in range(3)]
     two = [from_rows(1, a, two[a]) for a in range(3)]
 
-    for relays in one:
+    stores = []
+
+    def store(f, a, relays, out):
         for copy in relays:
             copy.wait_recv()
-    stores = [pltpu.make_async_copy(fin.at[0], g1_out, local.at[2])]
-    stores[0].start()
+        copy = pltpu.make_async_copy(fin.at[f, :, taps(a)], out.at[:, taps(a)], local.at[3 * f + a])
+        copy.start()
+        stores.append(copy)
+
+    for a in range(3):
+        store(0, a, one[a], g1_out)
     two = [to_other(1, a, two[a]) for a in range(3)]
     scattered(3, gf, gfin)
 
@@ -460,11 +480,8 @@
     def _(s):
         gf_out[s // R, lax.rem(s, R)] = summed(gf, gfin, s).astype(BF16)
 
-    for relays in two:
-        for copy in relays:
-            copy.wait_recv()
-    stores.append(pltpu.make_async_copy(fin.at[1], g2_out, local.at[3]))
-    stores[1].start()
+    for a in range(3):
+        store(1, a, two[a], g2_out)
 
     for go, copy in pending:
         if go is None:
@@ -491,6 +508,8 @@
     scratch = [
         pltpu.VMEM((9, 3 * C, CC), BF16),
         pltpu.VMEM((9, 3 * C, CC), BF16),
+        pltpu.VMEM((Z, 3 * C, 9 * C), BF16),
+        pltpu.VMEM((slabs // 2, 3 * C, 2 * J), F32),
         pltpu.VMEM(ext + (CC, J), BF16),
         pltpu.VMEM(ext + (C, J), BF16),
         pltpu.VMEM(ext + (3 * C, J), BF16),
@@ -541,12 +560,12 @@
                 wide[:, :, half * CC // 2 : (half + 1) * CC // 2] = narrow[half].astype(F32)
 
     cells = pl.BlockSpec((F, R, C, J), lambda a: (0, 0, 0, 0))
-    narrow = pl.BlockSpec((2, 3, 3 * C, CC // 2), lambda a: (0, a, 0, 0))
-    wide = pl.BlockSpec((3, 3 * C, CC), lambda a: (a, 0, 0))
+    narrow = pl.BlockSpec((2, 1, 3 * C, CC // 2), lambda a: (0, a, 0, 0))
+    wide = pl.BlockSpec((1, 3 * C, CC), lambda a: (a, 0, 0))
     filters = jax.ShapeDtypeStruct((9, 3 * C, CC), F32)
     grad_frames, one, two = pl.pallas_call(
         widened,
-        grid=(3,),
+        grid=(9,),
         out_shape=(jax.ShapeDtypeStruct((F, R, C, J), BF16), filters, filters),
         in_specs=[cells, narrow, narrow],
         out_specs=(cells, wide, wide),

time: 65.5 us -> 67.5 us (1.031)
  Pallas kernels: 64 us -> 66.1 us
    pallas_call x1, Pallas kernels: 3.85 us -> 6.53 us  [on_device(): pl.pallas_call(widened, grid=(9,), out_shape=(jax.ShapeDtypeStruct((F, R,...]
where the time goes in v4:
time: 67.5 us; the launch traced here: 66.7 us
  Pallas kernels  66.1 us (98%)
    pallas_call x1, Pallas kernels, on_device(): pl.pallas_call(functools.partial(kernel, sizes), out_shape=(jax.ShapeDtyp...  59.5 us
    pallas_call x1, Pallas kernels, on_device(): pl.pallas_call(widened, grid=(9,), out_shape=(jax.ShapeDtypeStruct((F, R,...  6.53 us

profile of v4, /device:TPU:0, one launch (start us, length us, event | category | flops | bytes accessed | tf_op | source)
XLA Modules:
  0.0 66.7 jit_solution(16308927571030831075)
XLA Ops:
  0.6 59.5 %shard_map.67 = (bf16[2,4,64,128]{3,2,1,0:T(8,128)(2,1)}, bf16[2,9,192,128]{3,2,1,0:T(8,128)(2,1)}, bf16[2,9,192,128]{3,2,1,0:T(8,128)(2,1)}) custom-call(bf16[2,4,64,128]{3,2,1,0:T(8,128)(2,1)} %frames.1, bf16[2,4,64,128]{3,2,1,0:T(8,128)(2,1)} %gout.1, bf16[9,192,256]{2,1,0:T(8,128)(2,1)} %bitcast.12, bf16[9,192,256]{2,1,0:T(8,128)(2,1)} %bitcast.13), custom_call_target="tpu_custom_call" | custom-call | tf_op jit(solution)/shard_map/pallas_call | solution.py:541
  60.2 6.5 %shard_map.68 = (bf16[2,4,64,128]{3,2,1,0:T(8,128)(2,1)}, f32[9,192,256]{2,1,0:T(8,128)}, f32[9,192,256]{2,1,0:T(8,128)}) custom-call(bf16[2,4,64,128]{3,2,1,0:T(8,128)(2,1)} %get-tuple-element.9.cells_in, bf16[2,9,192,128]{3,2,1,0:T(8,128)(2,1)} %get-tuple-element.10.one_in, bf16[2,9,192,128]{3,2,1,0:T(8,128)(2,1)} %get-tuple-element.11.two_in), custom_call_target="tpu_custom_call" | custom-call | tf_op jit(solution)/shard_map/pallas_call | solution.py:566

commit v5 on v3

--- a/solution.py
+++ b/solution.py
@@ -107,6 +107,15 @@
             def _(dst=dst, q=q):
                 dst[q] = jnp.zeros(dst.shape[1:], dst.dtype)
 
+    def turned(weight, out):
+        flat = weight[...].reshape(27 * O, CC)
+        for k in range(0, 27 * O, 2 * J):
+            end = min(k + 2 * J, 27 * O)
+            out[:, k:end] = flat[k:end].T
+
+    loads[0].wait()
+    turned(w2, w2t)
+
     n_t = jnp.where(has_prev, 1, 0) + jnp.where(has_next, 1, 0)
     n_h = jnp.where(up, 1, 0) + jnp.where(down, 1, 0)
     pl.semaphore_wait(barrier, (Z - 1) + (H - 1) + n_t + n_t * n_h)
@@ -178,12 +187,16 @@
         other = jnp.where(k < side, k, k + 1)
         return jnp.where(low, other, Z - 1 - other)
 
-    def gathered(phase, k, block):
+    def gathered(phase, k, block, unless=None):
         q = nearest(k)
-        remote(
+        landed = remote(
             block(q), block(q), z_send.at[phase, q], z_recv.at[phase, q], zpeer(1)
-        ).wait_recv()
-        if FAR < Z:
+        )
+        if unless is None:
+            landed.wait_recv()
+        else:
+            pl.when(jnp.logical_not(unless))(landed.wait_recv)
+        if FAR < Z and unless is None:
             for go, dz in (
                 (both(both(q < z, z < Z - 1), z + 1 - q >= FAR), 1),
                 (both(both(q > z, z > 0), q + 1 - z >= FAR), -1),
@@ -192,6 +205,23 @@
                     block(q), block(q), zz_send.at[phase, k], z_recv.at[phase, q], {"chan": z + dz}
                 ))
         return q
+
+    middle = both(z > 0, z < Z - 1)
+
+    def forwarded(phase, block):
+        if FAR < Z:
+            q = nearest(Z - 2)
+
+            @pl.when(middle)
+            def _():
+                remote(
+                    block(q), block(q), z_send.at[phase, q], z_recv.at[phase, q], zpeer(1)
+                ).wait_recv()
+
+            for go, dz in ((both(middle, q < z), 1), (both(middle, q > z), -1)):
+                send_if(go, remote(
+                    block(q), block(q), zz_send.at[phase, 0], z_recv.at[phase, q], {"chan": z + dz}
+                ))
 
     ends = (0, Z - 1) if FAR < Z else ()
 
@@ -257,15 +287,6 @@
     g_plan = halo_plan(g, -1, pl.ds(0, C), gh_send.at[0], gh_recv.at[0])
     depart(g_plan)
     depart(x_halo(z))
-    def turned(weight, out):
-        flat = weight[...].reshape(27 * O, CC)
-        for k in range(0, 27 * O, 2 * J):
-            end = min(k + 2 * J, 27 * O)
-            out[:, k:end] = flat[k:end].T
-
-    loads[0].wait()
-
-    turned(w2, w2t)
 
     def spread(src, dst, t, i):
         wide = src[t, i].astype(F32)
@@ -424,6 +445,7 @@
         return jnp.concatenate([act[s] for s in range(slabs)], 1)
 
     one = [to_pair(0, a, first_left, first_right) for a in range(3)]
+    forwarded(2, act_block)
     one = [to_rows(0, a, one[a]) for a in range(3)]
 
     arrive(gp_plan)
@@ -436,23 +458,29 @@
         for i in (0, R + 1):
             spread(gp, gpsh, t, i)
     back(gpsh, w1t, gf)
+    one = [from_rows(0, a, one[a]) for a in range(3)]
 
     for k in range(Z - 1):
-        gathered(2, k, act_block)
+        gathered(2, k, act_block, unless=both(middle, k == Z - 2) if FAR < Z else both(z < 0, z > 0))
     scatter(3, gf, gfin)
 
     two = [to_pair(1, a, second_left, second_right) for a in range(3)]
-    one = [from_rows(0, a, one[a]) for a in range(3)]
     two = [to_rows(1, a, two[a]) for a in range(3)]
     scatter_rest(3, gf, gfin)
     one = [to_other(0, a, one[a]) for a in range(3)]
     two = [from_rows(1, a, two[a]) for a in range(3)]
 
-    for relays in one:
+    stores = []
+
+    def store(f, a, relays, out):
         for copy in relays:
             copy.wait_recv()
-    stores = [pltpu.make_async_copy(fin.at[0], g1_out, local.at[2])]
-    stores[0].start()
+        copy = pltpu.make_async_copy(fin.at[f, :, taps(a)], out.at[:, taps(a)], local.at[3 * f + a])
+        copy.start()
+        stores.append(copy)
+
+    for a in range(3):
+        store(0, a, one[a], g1_out)
     two = [to_other(1, a, two[a]) for a in range(3)]
     scattered(3, gf, gfin)
 
@@ -460,11 +488,8 @@
     def _(s):
         gf_out[s // R, lax.rem(s, R)] = summed(gf, gfin, s).astype(BF16)
 
-    for relays in two:
-        for copy in relays:
-            copy.wait_recv()
-    stores.append(pltpu.make_async_copy(fin.at[1], g2_out, local.at[3]))
-    stores[1].start()
+    for a in range(3):
+        store(1, a, two[a], g2_out)
 
     for go, copy in pending:
         if go is None:
@@ -534,22 +559,47 @@
         ),
     )(frames, grad_out, taps_first(weight_one), taps_first(weight_two))
 
-    def widened(cells_in, one_in, two_in, cells_out, one_out, two_out):
-        cells_out[...] = cells_in[...]
-        for narrow, wide in ((one_in, one_out), (two_in, two_out)):
-            for half in range(2):
-                wide[:, :, half * CC // 2 : (half + 1) * CC // 2] = narrow[half].astype(F32)
-
-    cells = pl.BlockSpec((F, R, C, J), lambda a: (0, 0, 0, 0))
-    narrow = pl.BlockSpec((2, 3, 3 * C, CC // 2), lambda a: (0, a, 0, 0))
-    wide = pl.BlockSpec((3, 3 * C, CC), lambda a: (a, 0, 0))
-    filters = jax.ShapeDtypeStruct((9, 3 * C, CC), F32)
+    narrow, wide = (2, 9, 3 * C, CC // 2), (9, 3 * C, CC)
+
+    def widened(
+        cells_in, one_in, two_in, cells_out, one_out, two_out,
+        cells, narrow_one, narrow_two, wide_one, wide_two, arrived, left,
+    ):
+        both = ((one_in, narrow_one, wide_one, one_out), (two_in, narrow_two, wide_two, two_out))
+        fetch = []
+        for f, (source, near, _, _) in enumerate(both):
+            for a in range(3):
+                taps = pl.ds(3 * a, 3)
+                fetch.append(pltpu.make_async_copy(source.at[:, taps], near.at[:, taps], arrived.at[f, a]))
+        fetch.append(pltpu.make_async_copy(cells_in, cells, arrived.at[2, 0]))
+        for copy in fetch:
+            copy.start()
+        stores = []
+        for f, (_, near, far, out) in enumerate(both):
+            for a in range(3):
+                fetch[3 * f + a].wait()
+                for ab in range(3 * a, 3 * a + 3):
+                    for half in range(2):
+                        far[ab, :, half * CC // 2 : (half + 1) * CC // 2] = near[half, ab].astype(F32)
+                taps = pl.ds(3 * a, 3)
+                stores.append(pltpu.make_async_copy(far.at[taps], out.at[taps], left.at[f, a]))
+                stores[-1].start()
+        fetch[6].wait()
+        stores.append(pltpu.make_async_copy(cells, cells_out, left.at[2, 0]))
+        stores[-1].start()
+        for copy in stores:
+            copy.wait()
+
+    filters = jax.ShapeDtypeStruct(wide, F32)
     grad_frames, one, two = pl.pallas_call(
         widened,
-        grid=(3,),
         out_shape=(jax.ShapeDtypeStruct((F, R, C, J), BF16), filters, filters),
-        in_specs=[cells, narrow, narrow],
-        out_specs=(cells, wide, wide),
+        in_specs=[hbm] * 3,
+        out_specs=(hbm,) * 3,
+        scratch_shapes=[
+            pltpu.VMEM((F, R, C, J), BF16), pltpu.VMEM(narrow, BF16), pltpu.VMEM(narrow, BF16),
+            pltpu.VMEM(wide, F32), pltpu.VMEM(wide, F32), dma((3, 3)), dma((3, 3)),
+        ],
         compiler_params=pltpu.CompilerParams(vmem_limit_bytes=56 * 1024 * 1024),
     )(grad_frames, one, two)
 

time: 65.5 us -> 62.2 us (0.950)
  the two profiles are of different devices: /device:TPU:0 before, /device:TPU:17 now
where the time goes in v5:
time: 62.2 us; the launch traced here: 62 us
  Pallas kernels  61.4 us (99%)
  between operations  0.64 us (1%)
    pallas_call x1, Pallas kernels, on_device(): pl.pallas_call(functools.partial(kernel, sizes), out_shape=(jax.ShapeDtyp...  58.4 us
    pallas_call x1, Pallas kernels, on_device(): pl.pallas_call(widened, out_shape=(jax.ShapeDtypeStruct((F, R, C, J), BF1...  2.98 us

profile of v5, /device:TPU:17, one launch (start us, length us, event | category | flops | bytes accessed | tf_op | source)
XLA Modules:
  0.0 62.0 jit_solution(17539131505336344937)
XLA Ops:
  0.6 58.4 %shard_map.67 = (bf16[2,4,64,128]{3,2,1,0:T(8,128)(2,1)}, bf16[2,9,192,128]{3,2,1,0:T(8,128)(2,1)}, bf16[2,9,192,128]{3,2,1,0:T(8,128)(2,1)}) custom-call(bf16[2,4,64,128]{3,2,1,0:T(8,128)(2,1)} %frames.1, bf16[2,4,64,128]{3,2,1,0:T(8,128)(2,1)} %gout.1, bf16[9,192,256]{2,1,0:T(8,128)(2,1)} %bitcast.12, bf16[9,192,256]{2,1,0:T(8,128)(2,1)} %bitcast.13), custom_call_target="tpu_custom_call" | custom-call | tf_op jit(solution)/shard_map/pallas_call | solution.py:547
  59.1 3.0 %shard_map.68 = (bf16[2,4,64,128]{3,2,1,0:T(8,128)(2,1)}, f32[9,192,256]{2,1,0:T(8,128)}, f32[9,192,256]{2,1,0:T(8,128)}) custom-call(bf16[2,4,64,128]{3,2,1,0:T(8,128)(2,1)} %get-tuple-element.9.cells_in, bf16[2,9,192,128]{3,2,1,0:T(8,128)(2,1)} %get-tuple-element.10.one_in, bf16[2,9,192,128]{3,2,1,0:T(8,128)(2,1)} %get-tuple-element.11.two_in), custom_call_target="tpu_custom_call" | custom-call | tf_op jit(solution)/shard_map/pallas_call | solution.py:594

commit v6 on v5

--- a/solution.py
+++ b/solution.py
@@ -240,11 +240,13 @@
             src.at[:, pl.ds(p * C, C), :], dst.at[z], z_send.at[phase, p], z_recv.at[phase, z], {"chan": p}
         )
 
-    def scatter(phase, src, dst):
+    def scatter(phase, src, dst, only=None):
         for p in ends:
-            send_if(z == Z - 1 - p, passed(phase, src, p))
+            if only is not middle:
+                send_if(z == Z - 1 - p, passed(phase, src, p))
         for p in range(Z):
             go = both(near(p), jnp.logical_not(takes(p))) if p in ends else near(p)
+            go = go if only is None else both(go, only)
             pl.when(go)(direct(phase, src, dst, p).start)
 
     def scatter_rest(phase, src, dst):
@@ -342,8 +344,8 @@
             pre[2 * s + half] = value
             act[2 * s + half, mine, :] = (value * jax.nn.sigmoid(value)).astype(BF16)
 
+    gather(2, act_block)
     scattered(1, ga, gain)
-    gather(2, act_block)
 
     @pl.loop(0, slabs, unroll=4)
     def _(s):
@@ -370,10 +372,8 @@
     def taps(a):
         return pl.ds(3 * a, 3)
 
-    def to_pair(f, a, left_of, right_of):
-        @pl.loop(0, 3)
-        def _(b):
-            value = lax.dot_general(left_of(a, b), right_of(a, b), nt, preferred_element_type=F32)
+    def to_pair(f, a, values):
+        for b, value in enumerate(values):
             left, right = value[:, :J], value[:, J:]
             town[f, 3 * a + b] = jnp.where(parity == 0, left, right)
             tsend[f, 3 * a + b] = jnp.where(parity == 0, right, left).astype(BF16)
@@ -432,21 +432,21 @@
             relays.append(relay(f, a, d))
         return relays
 
-    def first_left(a, b):
-        return row_of(gpsh, 0, 1)
-
-    def first_right(a, b):
-        return row_of(x, a, b)
-
-    def second_left(a, b):
-        return row_of(gsh, 2 - a, 2 - b)
-
-    def second_right(a, b):
-        return jnp.concatenate([act[s] for s in range(slabs)], 1)
-
-    one = [to_pair(0, a, first_left, first_right) for a in range(3)]
+    def first_taps(a):
+        left = row_of(gpsh, 0, 1)
+        return [
+            lax.dot_general(left, row_of(x, a, b), nt, preferred_element_type=F32) for b in range(3)
+        ]
+
+    def second_taps(a):
+        left = jnp.concatenate([row_of(gsh, 2 - a, 2 - b) for b in range(3)], 0)
+        right = jnp.concatenate([act[s] for s in range(slabs)], 1)
+        value = lax.dot_general(left, right, nt, preferred_element_type=F32)
+        return [value[b * 3 * O : (b + 1) * 3 * O] for b in range(3)]
+
+    one = [to_pair(0, a, first_taps(a)) for a in range(3)]
+    one = [to_rows(0, a, one[a]) for a in range(3)]
     forwarded(2, act_block)
-    one = [to_rows(0, a, one[a]) for a in range(3)]
 
     arrive(gp_plan)
 
@@ -458,17 +458,18 @@
         for i in (0, R + 1):
             spread(gp, gpsh, t, i)
     back(gpsh, w1t, gf)
+    scatter(3, gf, gfin, only=jnp.logical_not(middle))
     one = [from_rows(0, a, one[a]) for a in range(3)]
 
     for k in range(Z - 1):
         gathered(2, k, act_block, unless=both(middle, k == Z - 2) if FAR < Z else both(z < 0, z > 0))
-    scatter(3, gf, gfin)
-
-    two = [to_pair(1, a, second_left, second_right) for a in range(3)]
+    scatter(3, gf, gfin, only=middle)
+
+    two = [to_pair(1, a, second_taps(a)) for a in range(3)]
     two = [to_rows(1, a, two[a]) for a in range(3)]
-    scatter_rest(3, gf, gfin)
     one = [to_other(0, a, one[a]) for a in range(3)]
     two = [from_rows(1, a, two[a]) for a in range(3)]
+    scatter_rest(3, gf, gfin)
 
     stores = []
 

time: 62.2 us -> 60.7 us (0.976)
  the two profiles are of different devices: /device:TPU:17 before, /device:TPU:0 now
where the time goes in v6:
time: 60.7 us; the launch traced here: 60.5 us
  Pallas kernels  59.9 us (99%)
  between operations  0.64 us (1%)
    pallas_call x1, Pallas kernels, on_device(): pl.pallas_call(functools.partial(kernel, sizes), out_shape=(jax.ShapeDtyp...  56.9 us
    pallas_call x1, Pallas kernels, on_device(): pl.pallas_call(widened, out_shape=(jax.ShapeDtypeStruct((F, R, C, J), BF1...  2.98 us

profile of v6, /device:TPU:0, one launch (start us, length us, event | category | flops | bytes accessed | tf_op | source)
XLA Modules:
  0.0 60.5 jit_solution(16378185832494049002)
XLA Ops:
  0.6 56.9 %shard_map.67 = (bf16[2,4,64,128]{3,2,1,0:T(8,128)(2,1)}, bf16[2,9,192,128]{3,2,1,0:T(8,128)(2,1)}, bf16[2,9,192,128]{3,2,1,0:T(8,128)(2,1)}) custom-call(bf16[2,4,64,128]{3,2,1,0:T(8,128)(2,1)} %frames.1, bf16[2,4,64,128]{3,2,1,0:T(8,128)(2,1)} %gout.1, bf16[9,192,256]{2,1,0:T(8,128)(2,1)} %bitcast.12, bf16[9,192,256]{2,1,0:T(8,128)(2,1)} %bitcast.13), custom_call_target="tpu_custom_call" | custom-call | tf_op jit(solution)/shard_map/pallas_call | solution.py:548
  57.6 3.0 %shard_map.68 = (bf16[2,4,64,128]{3,2,1,0:T(8,128)(2,1)}, f32[9,192,256]{2,1,0:T(8,128)}, f32[9,192,256]{2,1,0:T(8,128)}) custom-call(bf16[2,4,64,128]{3,2,1,0:T(8,128)(2,1)} %get-tuple-element.9.cells_in, bf16[2,9,192,128]{3,2,1,0:T(8,128)(2,1)} %get-tuple-element.10.one_in, bf16[2,9,192,128]{3,2,1,0:T(8,128)(2,1)} %get-tuple-element.11.two_in), custom_call_target="tpu_custom_call" | custom-call | tf_op jit(solution)/shard_map/pallas_call | solution.py:595

commit v7 on v6

--- a/solution.py
+++ b/solution.py
@@ -132,6 +132,13 @@
         pending.append((None, copy))
         return copy
 
+    def settle(sent):
+        for go, copy in sent:
+            if go is None:
+                copy.wait_send()
+            else:
+                pl.when(go)(copy.wait_send)
+
     def send_if(go, copy):
         pl.when(go)(copy.start)
         pending.append((go, copy))
@@ -296,8 +303,8 @@
         dst[t, i, O : 2 * O] = src[t, i]
         dst[t, i, 2 * O : 3 * O] = moved_cols(wide, -1).astype(BF16)
 
-    def back(source, weight, out):
-        @pl.loop(0, slabs // 2)
+    def back(source, weight, out, start=0, stop=slabs // 2):
+        @pl.loop(start, stop)
         def _(s):
             t, i = s // (R // 2), 2 * lax.rem(s, R // 2)
             windows = [
@@ -315,11 +322,15 @@
     def _(s):
         spread(g, gsh, s // (R + 2), lax.rem(s, R + 2))
 
-    back(gsh, w2t, ga)
+    depart(x_halo(gathered(0, 0, x_block)))
+    back(gsh, w2t, ga, 0, slabs // 4)
+    if Z > 2:
+        depart(x_halo(gathered(0, 1, x_block)))
+    back(gsh, w2t, ga, slabs // 4, slabs // 2)
     scatter(1, ga, gain)
     loads[1].wait()
 
-    for k in range(Z - 1):
+    for k in range(2, Z - 1):
         depart(x_halo(gathered(0, k, x_block)))
     scatter_rest(1, ga, gain)
 
@@ -444,8 +455,16 @@
         value = lax.dot_general(left, right, nt, preferred_element_type=F32)
         return [value[b * 3 * O : (b + 1) * 3 * O] for b in range(3)]
 
-    one = [to_pair(0, a, first_taps(a)) for a in range(3)]
-    one = [to_rows(0, a, one[a]) for a in range(3)]
+    def staggered(f, taps_of):
+        copies = [to_pair(f, 0, taps_of(0))]
+        rows = []
+        for a in range(1, 3):
+            copies.append(to_pair(f, a, taps_of(a)))
+            rows.append(to_rows(f, a - 1, copies[a - 1]))
+        rows.append(to_rows(f, 2, copies[2]))
+        return rows
+
+    one = staggered(0, first_taps)
     forwarded(2, act_block)
 
     arrive(gp_plan)
@@ -465,11 +484,14 @@
         gathered(2, k, act_block, unless=both(middle, k == Z - 2) if FAR < Z else both(z < 0, z > 0))
     scatter(3, gf, gfin, only=middle)
 
-    two = [to_pair(1, a, second_taps(a)) for a in range(3)]
-    two = [to_rows(1, a, two[a]) for a in range(3)]
+    drained = len(pending)
+    two = staggered(1, second_taps)
     one = [to_other(0, a, one[a]) for a in range(3)]
+    scatter_rest(3, gf, gfin)
     two = [from_rows(1, a, two[a]) for a in range(3)]
-    scatter_rest(3, gf, gfin)
+    settle(pending[:drained])
+    for plan in [g_plan, gp_plan] + [x_halo(q) for q in range(Z)]:
+        settle([(go, copy) for go, _, copy in plan])
 
     stores = []
 
@@ -492,14 +514,7 @@
     for a in range(3):
         store(1, a, two[a], g2_out)
 
-    for go, copy in pending:
-        if go is None:
-            copy.wait_send()
-        else:
-            pl.when(go)(copy.wait_send)
-    for plan in [g_plan, gp_plan] + [x_halo(q) for q in range(Z)]:
-        for go, _, copy in plan:
-            pl.when(go)(copy.wait_send)
+    settle(pending[drained:])
     for copy in stores:
         copy.wait()
 

time: 60.7 us -> 60.5 us (level)
  no operation moved by 1% of the time
where the time goes in v7:
time: 60.5 us; the launch traced here: 60.2 us
  Pallas kernels  59.6 us (99%)
  between operations  0.64 us (1%)
    pallas_call x1, Pallas kernels, on_device(): pl.pallas_call(functools.partial(kernel, sizes), out_shape=(jax.ShapeDtyp...  56.6 us
    pallas_call x1, Pallas kernels, on_device(): pl.pallas_call(widened, out_shape=(jax.ShapeDtypeStruct((F, R, C, J), BF1...  2.98 us

profile of v7, /device:TPU:0, one launch (start us, length us, event | category | flops | bytes accessed | tf_op | source)
XLA Modules:
  0.0 60.2 jit_solution(7542341296667076220)
XLA Ops:
  0.6 56.6 %shard_map.67 = (bf16[2,4,64,128]{3,2,1,0:T(8,128)(2,1)}, bf16[2,9,192,128]{3,2,1,0:T(8,128)(2,1)}, bf16[2,9,192,128]{3,2,1,0:T(8,128)(2,1)}) custom-call(bf16[2,4,64,128]{3,2,1,0:T(8,128)(2,1)} %frames.1, bf16[2,4,64,128]{3,2,1,0:T(8,128)(2,1)} %gout.1, bf16[9,192,256]{2,1,0:T(8,128)(2,1)} %bitcast.12, bf16[9,192,256]{2,1,0:T(8,128)(2,1)} %bitcast.13), custom_call_target="tpu_custom_call" | custom-call | tf_op jit(solution)/shard_map/pallas_call | solution.py:563
  57.3 3.0 %shard_map.68 = (bf16[2,4,64,128]{3,2,1,0:T(8,128)(2,1)}, f32[9,192,256]{2,1,0:T(8,128)}, f32[9,192,256]{2,1,0:T(8,128)}) custom-call(bf16[2,4,64,128]{3,2,1,0:T(8,128)(2,1)} %get-tuple-element.9.cells_in, bf16[2,9,192,128]{3,2,1,0:T(8,128)(2,1)} %get-tuple-element.10.one_in, bf16[2,9,192,128]{3,2,1,0:T(8,128)(2,1)} %get-tuple-element.11.two_in), custom_call_target="tpu_custom_call" | custom-call | tf_op jit(solution)/shard_map/pallas_call | solution.py:610

commit v8 on v7

--- a/solution.py
+++ b/solution.py
@@ -80,8 +80,10 @@
                 pl.semaphore_signal(
                     barrier, inc=1, device_id={"tm": tm + dt, "height": h + dh}, device_id_type=MESH
                 )
-    def near(p):
-        return both(z != p, jnp.abs(z - p) < FAR)
+    reach = (FAR, FAR, Z, Z)
+
+    def near(p, phase):
+        return both(z != p, jnp.abs(z - p) < reach[phase])
 
     def zero_edges(ext, dt):
         f0 = 0 if dt > 0 else F
@@ -101,9 +103,9 @@
     zero_edges(g, -1)
     zero_edges(gp, -1)
     zero_edges(x, 1)
-    for dst in (gain, gfin):
+    for dst, phase in ((gain, 1), (gfin, 3)):
         for q in range(Z):
-            @pl.when(jnp.logical_not(near(q)))
+            @pl.when(jnp.logical_not(near(q, phase)))
             def _(dst=dst, q=q):
                 dst[q] = jnp.zeros(dst.shape[1:], dst.dtype)
 
@@ -184,7 +186,7 @@
 
     def gather(phase, block):
         for p in sorted(range(Z), key=lambda p: abs(2 * p - Z + 1)):
-            send_if(near(p), remote(
+            send_if(near(p, phase), remote(
                 block(z), block(z), z_send.at[phase, p], z_recv.at[phase, z], {"chan": p}
             ))
 
@@ -203,7 +205,7 @@
             landed.wait_recv()
         else:
             pl.when(jnp.logical_not(unless))(landed.wait_recv)
-        if FAR < Z and unless is None:
+        if reach[phase] < Z and unless is None:
             for go, dz in (
                 (both(both(q < z, z < Z - 1), z + 1 - q >= FAR), 1),
                 (both(both(q > z, z > 0), q + 1 - z >= FAR), -1),
@@ -216,7 +218,7 @@
     middle = both(z > 0, z < Z - 1)
 
     def forwarded(phase, block):
-        if FAR < Z:
+        if reach[phase] < Z:
             q = nearest(Z - 2)
 
             @pl.when(middle)
@@ -230,7 +232,8 @@
                     block(q), block(q), zz_send.at[phase, 0], z_recv.at[phase, q], {"chan": z + dz}
                 ))
 
-    ends = (0, Z - 1) if FAR < Z else ()
+    def ends(phase):
+        return (0, Z - 1) if reach[phase] < Z else ()
 
     def takes(p):
         return z == (1 if p == Z - 1 else Z - 2)
@@ -248,16 +251,17 @@
         )
 
     def scatter(phase, src, dst, only=None):
-        for p in ends:
+        for p in ends(phase):
             if only is not middle:
                 send_if(z == Z - 1 - p, passed(phase, src, p))
         for p in range(Z):
-            go = both(near(p), jnp.logical_not(takes(p))) if p in ends else near(p)
+            go = near(p, phase)
+            go = both(go, jnp.logical_not(takes(p))) if p in ends(phase) else go
             go = go if only is None else both(go, only)
             pl.when(go)(direct(phase, src, dst, p).start)
 
     def scatter_rest(phase, src, dst):
-        for p in ends:
+        for p in ends(phase):
             @pl.when(takes(p))
             def _(p=p):
                 passed(phase, src, p).wait_recv()
@@ -267,11 +271,11 @@
                 ).astype(BF16)
                 direct(phase, src, dst, p).start()
         for p in range(Z):
-            pending.append((near(p), direct(phase, src, dst, p)))
+            pending.append((near(p, phase), direct(phase, src, dst, p)))
 
     def scattered(phase, src, dst):
         for q in range(Z):
-            pl.when(near(q))(remote(
+            pl.when(near(q, phase))(remote(
                 src.at[:, pl.ds(0, C), :], dst.at[q], z_send.at[phase, q], z_recv.at[phase, q], zpeer(1)
             ).wait_recv)
 
@@ -477,12 +481,11 @@
         for i in (0, R + 1):
             spread(gp, gpsh, t, i)
     back(gpsh, w1t, gf)
-    scatter(3, gf, gfin, only=jnp.logical_not(middle))
+    scatter(3, gf, gfin)
     one = [from_rows(0, a, one[a]) for a in range(3)]
 
     for k in range(Z - 1):
-        gathered(2, k, act_block, unless=both(middle, k == Z - 2) if FAR < Z else both(z < 0, z > 0))
-    scatter(3, gf, gfin, only=middle)
+        gathered(2, k, act_block, unless=both(middle, k == Z - 2) if reach[2] < Z else None)
 
     drained = len(pending)
     two = staggered(1, second_taps)

time: 60.5 us -> 61.1 us (level)
  Pallas kernels: 59.6 us -> 60.3 us
    pallas_call x1, Pallas kernels: 56.6 us -> 57.3 us  [on_device(): pl.pallas_call(functools.partial(kernel, sizes), out_shape=(jax.ShapeDtyp...]
where the time goes in v8:
time: 61.1 us; the launch traced here: 60.9 us
  Pallas kernels  60.3 us (99%)
  between operations  0.64 us (1%)
    pallas_call x1, Pallas kernels, on_device(): pl.pallas_call(functools.partial(kernel, sizes), out_shape=(jax.ShapeDtyp...  57.3 us
    pallas_call x1, Pallas kernels, on_device(): pl.pallas_call(widened, out_shape=(jax.ShapeDtypeStruct((F, R, C, J), BF1...  2.98 us

profile of v8, /device:TPU:0, one launch (start us, length us, event | category | flops | bytes accessed | tf_op | source)
XLA Modules:
  0.0 60.9 jit_solution(4179614977783989726)
XLA Ops:
  0.6 57.3 %shard_map.67 = (bf16[2,4,64,128]{3,2,1,0:T(8,128)(2,1)}, bf16[2,9,192,128]{3,2,1,0:T(8,128)(2,1)}, bf16[2,9,192,128]{3,2,1,0:T(8,128)(2,1)}) custom-call(bf16[2,4,64,128]{3,2,1,0:T(8,128)(2,1)} %frames.1, bf16[2,4,64,128]{3,2,1,0:T(8,128)(2,1)} %gout.1, bf16[9,192,256]{2,1,0:T(8,128)(2,1)} %bitcast.12, bf16[9,192,256]{2,1,0:T(8,128)(2,1)} %bitcast.13), custom_call_target="tpu_custom_call" | custom-call | tf_op jit(solution)/shard_map/pallas_call | solution.py:566
  57.9 3.0 %shard_map.68 = (bf16[2,4,64,128]{3,2,1,0:T(8,128)(2,1)}, f32[9,192,256]{2,1,0:T(8,128)}, f32[9,192,256]{2,1,0:T(8,128)}) custom-call(bf16[2,4,64,128]{3,2,1,0:T(8,128)(2,1)} %get-tuple-element.9.cells_in, bf16[2,9,192,128]{3,2,1,0:T(8,128)(2,1)} %get-tuple-element.10.one_in, bf16[2,9,192,128]{3,2,1,0:T(8,128)(2,1)} %get-tuple-element.11.two_in), custom_call_target="tpu_custom_call" | custom-call | tf_op jit(solution)/shard_map/pallas_call | solution.py:613
